TPU v7x, 128 devices: a whole 4x4x4 slice. The times are simulated.
128 devices in a mesh: wide: 16 (over z_lo, y, core), narrow: 8 (over x, z_hi).
Axes of the slice: x: 4, y: 4, z: 4 (z_hi: 2, z_lo: 2; z = z_hi * 2 + z_lo), core: 2. Of those that a mesh axis runs over, the one named last changes fastest.
Arguments:
- tokens: bfloat16 [512, 16384], P('wide', 'narrow'), may hold values from -6 to 6
- gate_codes: bfloat16 [16384, 26624], P('narrow', 'wide'), may hold values from -8 to 7, as said below
- up_codes: bfloat16 [16384, 26624], P('narrow', 'wide'), may hold values from -8 to 7, as said below
- gate_scale: float32 [128, 26624], P('narrow', 'wide'), may hold values from 0.0009 to 0.003
- up_scale: float32 [128, 26624], P('narrow', 'wide'), may hold values from 0.0009 to 0.003
- down_codes: bfloat16 [26624, 16384], P('wide', 'narrow'), may hold values from -8 to 7, as said below
- down_scale: float32 [208, 16384], P('wide', 'narrow'), may hold values from 0.0007 to 0.0024
- gate_left: float32 [16384, 128], P('narrow'), may hold values from -0.046875 to 0.046875
- gate_right: float32 [128, 26624], P(None, 'wide'), may hold values from -0.5 to 0.5
- up_left: float32 [16384, 128], P('narrow'), may hold values from -0.046875 to 0.046875
- up_right: float32 [128, 26624], P(None, 'wide'), may hold values from -0.5 to 0.5
- down_left: float32 [26624, 128], P('wide'), may hold values from -0.0390625 to 0.0390625
- down_right: float32 [128, 16384], P(None, 'narrow'), may hold values from -0.5 to 0.5
Outputs:
- mixed: float32 [512, 16384], P('wide', 'narrow')
Inputs may be any that keep to these rules, and one draw needn't show every extreme that they name: `gate_codes`: integer values. `up_codes`: integer values. `down_codes`: integer values.
All inputs are finite; a program needn't handle non-finite values.
Results may differ from a plain program's by a relative error of at most 0.011.
Values may be sent and summed in bfloat16 or wider, within the bound.
A program may use at most 128 MiB of HBM per device.

v0:
```python
import jax
import jax.numpy as jnp
from jax import lax
from jax.sharding import PartitionSpec as P


def dequant(codes, scale):
    rows, cols = codes.shape
    groups = scale.shape[0]
    values = codes.astype(jnp.float32).reshape(groups, rows // groups, cols) * scale[:, None, :]
    return values.reshape(rows, cols).astype(jnp.bfloat16)


def split_parts(factor):
    factor_high = factor.astype(jnp.bfloat16)
    factor_rest = (factor - factor_high.astype(jnp.float32)).astype(jnp.bfloat16)
    return (factor_high, factor_rest)


def shards(
    tokens,
    gate_codes,
    up_codes,
    gate_scale,
    up_scale,
    down_codes,
    down_scale,
    gate_left,
    gate_right,
    up_left,
    up_right,
    down_left,
    down_right,
):
    highest = lax.Precision.HIGHEST
    columns = gate_codes.shape[1]
    rank_cols = gate_left.shape[1]
    tok_rows = tokens.shape[0]
    gate_high, gate_rest = split_parts(gate_left)
    up_high, up_rest = split_parts(up_left)
    both_w = jnp.concatenate(
        [
            dequant(gate_codes, gate_scale),
            dequant(up_codes, up_scale),
            gate_high,
            up_high,
            gate_rest,
            up_rest,
        ],
        axis=1,
    )
    low_start = 2 * columns
    full = jnp.dot(
        lax.all_gather(tokens, "wide", axis=0, tiled=True),
        both_w,
        preferred_element_type=jnp.float32,
    )
    lowered = full[:, low_start : low_start + 2 * rank_cols] + full[:, low_start + 2 * rank_cols :]
    partial_rows = jnp.concatenate([full[:, :low_start], lowered], axis=1)
    summed = lax.psum(partial_rows, "narrow")
    gate = summed[:, :columns] + jnp.dot(
        summed[:, 2 * columns : 2 * columns + rank_cols], gate_right, precision=highest
    )
    up_val = summed[:, columns : 2 * columns] + jnp.dot(
        summed[:, 2 * columns + rank_cols :], up_right, precision=highest
    )
    hidden = (jax.nn.silu(gate) * up_val).astype(jnp.bfloat16)
    down_w = dequant(down_codes, down_scale)
    down_high, down_rest = split_parts(down_left)
    both_low = jnp.dot(
        hidden, jnp.concatenate([down_high, down_rest], axis=1), preferred_element_type=jnp.float32
    )
    middle = lax.psum(both_low[:, :rank_cols] + both_low[:, rank_cols:], "wide")
    own_mid = lax.dynamic_slice_in_dim(middle, lax.axis_index("wide") * tok_rows, tok_rows, 0)
    lowered = jnp.dot(own_mid, down_right, precision=highest)
    return (
        lax.psum_scatter(
            jnp.dot(hidden, down_w, preferred_element_type=jnp.float32),
            "wide",
            scatter_dimension=0,
            tiled=True,
        )
        + lowered
    )


def solution(mesh):
    placed = (
        P("wide", "narrow"),
        P("narrow", "wide"),
        P("narrow", "wide"),
        P("narrow", "wide"),
        P("narrow", "wide"),
        P("wide", "narrow"),
        P("wide", "narrow"),
        P("narrow", None),
        P(None, "wide"),
        P("narrow", None),
        P(None, "wide"),
        P("wide", None),
        P(None, "narrow"),
    )
    return jax.shard_map(
        shards, mesh=mesh, in_specs=placed, out_specs=P("wide", "narrow"), check_vma=False
    )
```

profile of v0, /device:TPU:1, one launch (start us, length us, event | category | flops | bytes accessed | tf_op | source)
XLA Modules:
  0.0 575.1 jit_solution(10940280249596445684)
XLA Ops:
  6.5 0.7 all-gather.2.cloned.1.call-update
  7.3 0.0 all-reduce.3.cloned.1.call-start
  7.3 7.1 %constant_dynamic-update-slice_fusion.1 = bf16[2048,3840]{1,0:T(8,128)(2,1)} fusion(f32[16,1664]{1,0:T(8,128)} %param.16, bf16[2048,1664]{1,0:T(8,128)(2,1)} %param.14), kind=kLoop, calls=%fused_computation.31 | loop fusion | flops 10223615 | bytes 13737984
  14.5 0.0 copy-start.3
  14.5 4.4 constant_dynamic-update-slice_fusion
  18.9 0.9 convert_dynamic-update-slice_fusion.1
  19.8 0.9 convert_dynamic-update-slice_fusion
  20.8 0.9 fusion.9
  21.7 1.0 fusion.10
  22.7 23.9 %all-gather.2.cloned.1.call-done = bf16[512,2048]{1,0:T(8,128)(2,1)} async-done(((bf16[32,2048]{1,0:T(8,128)(2,1)}), bf16[512,2048]{1,0:T(8,128)(2,1)}) %all-gather.2.cloned.1.call-update) | async-done | bytes 2097168 | tf_op jit(solution)/shard_map/all_gather | solution.py:54
  46.6 12.1 %convolution_bitcast_fusion = f32[512,3840]{0,1:T(8,128)S(1)} fusion(bf16[2048,3840]{1,0:T(8,128)(2,1)} %fusion.10, bf16[512,2048]{1,0:T(8,128)(2,1)} %all-gather.2.cloned.1.call-done), kind=kOutput, calls=%fused_computation.7 | convolution fusion | flops 8053063680 | bytes 25690112 | tf_op jit(solution)/shard_map/dot_general | solution.py:53
  58.7 0.8 slice.36
  59.5 0.1 slice_add_fusion.2
  59.6 3.8 pad_maximum_fusion
  63.4 0.0 all-reduce.3.cloned.1.call-update
  63.4 0.0 copy-start.6
  63.4 0.2 all-reduce.5.cloned.1.call-start
  63.7 0.6 copy-done.7
  64.3 8.2 %fusion = bf16[1664,2048]{1,0:T(8,128)(2,1)} fusion(bf16[1664,2048]{1,0:T(8,128)(2,1)} %param.18, f32[13,2048]{1,0:T(8,128)S(1)} %copy-done.7), kind=kLoop, calls=%fused_computation.1 | loop fusion | flops 10223616 | bytes 13737984 | tf_op jit(solution)/shard_map/convert_element_type | solution.py:11
  72.5 0.9 subtract_convert_fusion.2
  73.4 293.0 %all-reduce.3.cloned.1.call-done = f32[512,3584]{0,1:T(8,128)} async-done(((f32[512,3584]{0,1:T(8,128)}), f32[512,3584]{0,1:T(8,128)}) %all-reduce.3.cloned.1.call-update) | async-done | bytes 7340048 | tf_op jit(solution)/shard_map/psum | solution.py:60
  366.4 3.8 fusion.12
  370.2 7.1 %fusion.4 = bf16[512,1664]{0,1:T(8,128)(2,1)S(1)} fusion(f32[512,3584]{0,1:T(8,128)} %all-reduce.3.cloned.1.call-done, f32[512,1664]{0,1:T(8,128)S(1)} %fusion.12, f32[128,1664]{1,0:T(8,128)} %param.23), kind=kOutput, calls=%fused_computation.10 | convolution fusion | flops 1315438592 | bytes 13041664 | tf_op jit(solution)/shard_map/dot_general | solution.py:64
  377.3 0.7 fusion.5
  378.0 0.7 slice_add_fusion.3
  378.7 0.0 all-reduce.5.cloned.1.call-update
  378.7 0.0 reduce-scatter.2.cloned.1.call-start
  378.8 8.5 %fusion.17 = f32[512,2048]{1,0:T(8,128)} fusion(bf16[512,1664]{0,1:T(8,128)(2,1)S(1)} %fusion.4, bf16[1664,2048]{1,0:T(8,128)(2,1)} %fusion), kind=kOutput, calls=%fused_computation.34 | convolution fusion | flops 3489660928 | bytes 12713984 | tf_op jit(solution)/shard_map/dot_general | solution.py:78
  387.3 0.0 reduce-scatter.2.cloned.1.call-update
  387.3 112.6 %all-reduce.5.cloned.1.call-done = f32[512,128]{1,0:T(8,128)} async-done(((f32[512,128]{1,0:T(8,128)}), f32[512,128]{1,0:T(8,128)}) %all-reduce.5.cloned.1.call-update) | async-done | bytes 262160 | tf_op jit(solution)/shard_map/psum | solution.py:73
  499.9 66.3 %reduce-scatter.2.cloned.1.call-done = f32[32,2048]{1,0:T(8,128)} async-done(((f32[512,2048]{1,0:T(8,128)}), f32[32,2048]{1,0:T(8,128)}) %reduce-scatter.2.cloned.1.call-update) | async-done | bytes 262160 | tf_op jit(solution)/shard_map/reduce_scatter | solution.py:77
  566.2 2.3 convolution_add_fusion
  (16 shorter events, 0.0 us)
Async XLA Ops:
  6.5 559.7 %copy-start = (f32[128,2048]{1,0:T(8,128)S(1)}, f32[128,2048]{1,0:T(8,128)}, u32[]{:S(2)}) copy-start(f32[128,2048]{1,0:T(8,128)} %param.25) | copy-start | bytes 3145732
  6.5 40.0 %all-gather.2.cloned.1.call-start = ((), (), s32[]{:S(2)}) async-start(), calls=%async_computation.1 | async-start | bytes 2228224 | tf_op jit(solution)/shard_map/all_gather | solution.py:54
  7.3 7.2 %copy-start.8 = (f32[16,1664]{1,0:T(8,128)S(1)}, f32[16,1664]{1,0:T(8,128)}, u32[]{:S(2)}) copy-start(f32[16,1664]{1,0:T(8,128)} %param.17) | copy-start | bytes 319492
  7.3 359.1 %all-reduce.3.cloned.1.call-start = ((), (), s32[]{:S(2)}) async-start(), calls=%async_computation.2 | async-start | bytes 14680064 | tf_op jit(solution)/shard_map/psum | solution.py:60
  7.3 7.2 %copy-start.1 = (bf16[2048,1664]{1,0:T(8,128)(2,1)S(1)}, bf16[2048,1664]{1,0:T(8,128)(2,1)}, u32[]{:S(2)}) copy-start(bf16[2048,1664]{1,0:T(8,128)(2,1)} %param.15) | copy-start | bytes 20447236
  14.5 4.4 copy-start.2
  14.5 5.4 copy-start.3
  63.4 0.9 copy-start.7
  63.4 9.1 %copy-start.5 = (f32[1664,128]{1,0:T(8,128)S(1)}, f32[1664,128]{1,0:T(8,128)}, u32[]{:S(2)}) copy-start(f32[1664,128]{1,0:T(8,128)} %param.24) | copy-start | bytes 2555908
  63.4 302.9 %copy-start.6 = (f32[128,1664]{1,0:T(8,128)S(1)}, f32[128,1664]{1,0:T(8,128)}, u32[]{:S(2)}) copy-start(f32[128,1664]{1,0:T(8,128)} %param.21) | copy-start | bytes 2555908
  63.4 436.5 %all-reduce.5.cloned.1.call-start = ((), (), s32[]{:S(2)}) async-start(), calls=%async_computation.4 | async-start | bytes 524288 | tf_op jit(solution)/shard_map/psum | solution.py:73
  370.2 7.1 %copy-start.4 = (bf16[1664,128]{1,0:T(8,128)(2,1)S(1)}, bf16[1664,128]{1,0:T(8,128)(2,1)}, u32[]{:S(2)}) copy-start(bf16[1664,128]{1,0:T(8,128)(2,1)} %get-tuple-element.6) | copy-start | bytes 1277956
  378.7 187.5 %reduce-scatter.2.cloned.1.call-start = ((), (), s32[]{:S(2)}) async-start(), calls=%async_computation.3 | async-start | bytes 4456448 | tf_op jit(solution)/shard_map/reduce_scatter | solution.py:77
Sparse Core Ops, SparseCore 0:
  9.1 37.4 all-gather.1
  63.5 302.7 all-reduce.2
  378.9 121.0 all-reduce.4
  502.3 63.8 reduce-scatter.1
where the time goes:
time: 579 us; the launch traced here: 575 us
  waiting for transfers between devices  497 us (86%)
  matrix products  34.5 us (6%)
  other arithmetic  29.1 us (5%)
  between operations  13.2 us (2%)
    psum x1, waiting for transfers between devices, shards(): summed = lax.psum(partial_rows, 'narrow')  293 us
    psum x1, waiting for transfers between devices, shards(): middle = lax.psum(both_low[:, :rank_cols] + both_low[:, rank_cols:], 'wide')  113 us
    reduce_scatter x1, waiting for transfers between devices, shards(): lax.psum_scatter(jnp.dot(hidden, down_w, preferred_element_type=jnp.float...  66.3 us
    all_gather x1, waiting for transfers between devices, shards(): lax.all_gather(tokens, 'wide', axis=0, tiled=True)  23.9 us
    unnamed x5, other arithmetic  14.3 us
    dot_general x1, matrix products, shards(): jnp.dot(lax.all_gather(tokens, 'wide', axis=0, tiled=True), both_w, prefe...  12.1 us
  transfers between devices with their start and end apart: 4, of which 4 were waited for; matrix products, arithmetic and copies ran while one was open for 6% of the time, Pallas kernels for 0%

commit v1 on v0

v1 whole, which is shorter than its diff:
```python
import jax
import jax.numpy as jnp
from jax import lax
from jax.experimental import pallas as pl
from jax.experimental.pallas import tpu as pltpu
from jax.sharding import PartitionSpec as P

MESH = pl.DeviceIdType.MESH
F32 = jnp.float32
BF16 = jnp.bfloat16
LANE = 128
HALVES = 2
SKEW_SUM = 2
SKEW_DOWN = 5


def remote(src, dst, send_sem, recv_sem, device):
    return pltpu.make_async_remote_copy(
        src_ref=src,
        dst_ref=dst,
        send_sem=send_sem,
        recv_sem=recv_sem,
        device_id=device,
        device_id_type=MESH,
    )


def aligned(value, size):
    return pl.multiple_of(value, size)


def make_kernel(n_wide, n_narrow, depth, columns, tok_rows):
    blocks = columns // LANE
    units = HALVES * blocks
    chips = n_wide // 2
    part = tok_rows // HALVES
    core_rows = chips * part
    half_rows = 2 * core_rows
    own_rows = half_rows // n_narrow
    groups = depth // LANE
    wide_k = depth + 2 * LANE

    def kernel(
        tok, gate_codes, up_codes, gate_scale, up_scale, down_codes, down_scale,
        gate_left, gate_right, up_left, up_right, down_left, down_right,
        out,
        x_all, w_up, w_down, partial, landed, hidden, acc,
        core_send, core_land, out_send, out_land,
        scale_v, dscale_v, left_v, right_v, dleft_v, dright_v, left_b, dright_b,
        load_w, load_d, load_s,
        tok_send, tok_recv, pair_send, pair_recv,
        sum_send, sum_recv, hid_send, hid_recv,
        core_ss, core_rs, out_ss, out_rs,
    ):
        w = lax.axis_index("wide")
        n = lax.axis_index("narrow")
        chip, core = w // 2, lax.rem(w, 2)
        sibling = (chip * 2 + (1 - core), n)

        def wide_peer(d):
            return lax.rem(chip + d, chips)

        def narrow_peer(d):
            return lax.rem(n + d, n_narrow)

        small = [
            pltpu.make_async_copy(gate_left, left_v.at[0], load_s.at[0]),
            pltpu.make_async_copy(up_left, left_v.at[1], load_s.at[1]),
            pltpu.make_async_copy(gate_scale, scale_v.at[0], load_s.at[2]),
            pltpu.make_async_copy(up_scale, scale_v.at[1], load_s.at[3]),
            pltpu.make_async_copy(gate_right, right_v.at[0], load_s.at[4]),
            pltpu.make_async_copy(up_right, right_v.at[1], load_s.at[5]),
            pltpu.make_async_copy(down_scale, dscale_v, load_s.at[6]),
            pltpu.make_async_copy(down_left, dleft_v, load_s.at[7]),
            pltpu.make_async_copy(down_right, dright_v, load_s.at[8]),
        ]

        def cols_of(g):
            return pl.ds(aligned(g * LANE, LANE), LANE)

        def up_loads(g):
            return [
                pltpu.make_async_copy(
                    codes.at[:, cols_of(g)],
                    w_up.at[g, pl.ds(0, depth), pl.ds(i * LANE, LANE)],
                    load_w.at[i, g],
                )
                for i, codes in enumerate((gate_codes, up_codes))
            ]

        def down_load(g):
            return pltpu.make_async_copy(
                down_codes.at[cols_of(g), :],
                w_down.at[cols_of(g), pl.ds(0, depth)],
                load_d.at[g],
            )

        for copy in small[:6]:
            copy.start()

        @pl.loop(0, blocks)
        def _(g):
            for copy in up_loads(g):
                copy.start()

        for copy in small[6:]:
            copy.start()

        @pl.loop(0, blocks)
        def _(g):
            down_load(g).start()

        barrier = pltpu.get_barrier_semaphore()
        for d in range(1, n_narrow):
            pl.semaphore_signal(barrier, inc=1, device_id=(w, narrow_peer(d)), device_id_type=MESH)
        for d in range(1, chips):
            pl.semaphore_signal(
                barrier, inc=1, device_id=(wide_peer(d) * 2 + core, n), device_id_type=MESH
            )
        pl.semaphore_signal(barrier, inc=1, device_id=sibling, device_id_type=MESH)
        pl.semaphore_wait(barrier, n_narrow - 1 + chips - 1 + 1)

        base = core * core_rows
        feats = pl.ds(0, depth)
        place = pl.ds(aligned(base + chip * part, 16), part)
        for h in range(HALVES):
            for d in range(1, chips):
                remote(
                    tok.at[pl.ds(h * part, part), :],
                    x_all.at[h, place, feats],
                    tok_send.at[h],
                    tok_recv.at[h],
                    (wide_peer(d) * 2 + core, n),
                ).start()
        for h in range(HALVES):
            x_all[h, place, feats] = tok[pl.ds(h * part, part), :]
        acc[...] = jnp.zeros_like(acc)

        for copy in small[:6]:
            copy.wait()
        left_b[:, pl.ds(0, LANE)] = left_v[0].astype(BF16)
        left_b[:, pl.ds(LANE, LANE)] = left_v[1].astype(BF16)

        @pl.loop(0, blocks)
        def _(g):
            for copy in up_loads(g):
                copy.wait()
            for i in range(2):
                here = pl.ds(i * LANE, LANE)
                for k in range(groups):
                    rows = pl.ds(k * LANE, LANE)
                    scale = scale_v[i, pl.ds(k, 1), cols_of(g)]
                    w_up[g, rows, here] = (w_up[g, rows, here].astype(F32) * scale).astype(BF16)
                right = right_v[i, :, cols_of(g)].astype(BF16)
                w_up[g, pl.ds(depth + i * LANE, LANE), here] = right
                w_up[g, pl.ds(depth + (1 - i) * LANE, LANE), here] = jnp.zeros_like(right)

        for copy in small[6:]:
            copy.wait()
        dright_b[...] = dright_v[...].astype(BF16)

        @pl.loop(0, blocks)
        def _(g):
            down_load(g).wait()
            rows = cols_of(g)
            scale = dscale_v[pl.ds(g, 1), :]
            w_down[rows, feats] = (w_down[rows, feats].astype(F32) * scale).astype(BF16)
            w_down[rows, pl.ds(depth, LANE)] = dleft_v[rows, :].astype(BF16)

        def pair_copy(h):
            rows = x_all.at[h, pl.ds(aligned(base, core_rows), core_rows), feats]
            return remote(rows, rows, pair_send.at[h], pair_recv.at[h], sibling)

        def tokens_in(h):
            got = x_all.at[h, pl.ds(0, (chips - 1) * part), feats]
            remote(got, got, tok_send.at[h], tok_recv.at[h], sibling).wait_recv()
            pair_copy(h).start()

        def low_rank(h):
            pair_copy(h).wait_recv()
            x_all[h, :, pl.ds(depth, 2 * LANE)] = jnp.dot(
                x_all[h, :, feats], left_b[...], preferred_element_type=F32
            ).astype(BF16)

        def first(u):
            h, g = u // blocks, lax.rem(u, blocks)
            partial[u] = jnp.dot(x_all[h], w_up[g], preferred_element_type=F32).astype(BF16)
            for d in range(1, n_narrow):
                peer = narrow_peer(d)
                remote(
                    partial.at[u, pl.ds(aligned(peer * own_rows, own_rows), own_rows)],
                    landed.at[u, d - 1],
                    sum_send.at[u],
                    sum_recv.at[u],
                    (w, peer),
                ).start()

        mine = pl.ds(aligned(n * own_rows, own_rows), own_rows)

        def summed(u):
            remote(landed.at[u], landed.at[u], sum_send.at[u], sum_recv.at[u], sibling).wait()
            total = partial[u, mine, :].astype(F32)
            for d in range(n_narrow - 1):
                total = total + landed[u, d].astype(F32)
            gate, up = total[:, :LANE], total[:, LANE:]
            hidden[u, mine, :] = (gate / (1.0 + jnp.exp(-gate)) * up).astype(BF16)
            for d in range(1, n_narrow):
                remote(
                    hidden.at[u, mine],
                    hidden.at[u, mine],
                    hid_send.at[u],
                    hid_recv.at[u],
                    (w, narrow_peer(d)),
                ).start()

        def second(u):
            h, g = u // blocks, lax.rem(u, blocks)
            got = hidden.at[u, pl.ds(0, half_rows - own_rows)]
            remote(got, got, hid_send.at[u], hid_recv.at[u], sibling).wait()
            acc[h] += jnp.dot(hidden[u], w_down[cols_of(g), :], preferred_element_type=F32)

        ours = pl.ds(aligned(base, core_rows), core_rows)
        theirs = pl.ds(aligned((1 - core) * core_rows, core_rows), core_rows)

        def core_copy(h):
            return remote(core_send.at[h], core_land.at[h], core_ss.at[h], core_rs.at[h], sibling)

        def to_sibling(h):
            low = acc[h, :, pl.ds(depth, LANE)].astype(BF16)
            acc[h, :, feats] += jnp.dot(low, dright_b[...], preferred_element_type=F32)
            core_send[h] = acc[h, theirs, feats].astype(BF16)
            core_copy(h).start()

        def to_owners(h):
            core_copy(h).wait()
            both = acc[h, ours, feats] + core_land[h].astype(F32)
            acc[h, ours, feats] = both
            out_send[h] = both.astype(BF16)
            for d in range(1, chips):
                peer = wide_peer(d)
                remote(
                    out_send.at[h, pl.ds(aligned(peer * part, part), part)],
                    out_land.at[h, d - 1],
                    out_ss.at[h],
                    out_rs.at[h],
                    (peer * 2 + core, n),
                ).start()

        def finish(h):
            remote(out_land.at[h], out_land.at[h], out_ss.at[h], out_rs.at[h], sibling).wait()
            total = acc[h, place, feats]
            for d in range(chips - 1):
                total = total + out_land[h, d].astype(F32)
            out[pl.ds(h * part, part), :] = total

        for h in range(HALVES):
            tokens_in(h)
            if h == 0:
                low_rank(h)

        @pl.loop(0, units + SKEW_DOWN)
        def _(t):
            @pl.when(t == blocks - 1)
            def _():
                low_rank(1)

            @pl.when(t < units)
            def _():
                first(t)

            @pl.when((t >= SKEW_SUM) & (t < units + SKEW_SUM))
            def _():
                summed(t - SKEW_SUM)

            @pl.when(t >= SKEW_DOWN)
            def _():
                second(t - SKEW_DOWN)

            @pl.when(t == blocks - 1 + SKEW_DOWN)
            def _():
                to_sibling(0)

            @pl.when(t == blocks + 1 + SKEW_DOWN)
            def _():
                to_owners(0)

        to_sibling(1)
        finish(0)
        to_owners(1)
        finish(1)
        for h in range(HALVES):
            got = x_all.at[h, pl.ds(0, (chips - 1) * part), feats]
            remote(got, got, tok_send.at[h], tok_recv.at[h], sibling).wait_send()
            pair_copy(h).wait_send()

    vmem = pltpu.VMEM
    dma = pltpu.SemaphoreType.DMA
    scratch = [
        vmem((HALVES, half_rows, wide_k), BF16),
        vmem((blocks, wide_k, 2 * LANE), BF16),
        vmem((columns, depth + LANE), BF16),
        vmem((units, half_rows, 2 * LANE), BF16),
        vmem((units, n_narrow - 1, own_rows, 2 * LANE), BF16),
        vmem((units, half_rows, LANE), BF16),
        vmem((HALVES, half_rows, depth + LANE), F32),
        vmem((HALVES, core_rows, depth), BF16),
        vmem((HALVES, core_rows, depth), BF16),
        vmem((HALVES, core_rows, depth), BF16),
        vmem((HALVES, chips - 1, part, depth), BF16),
        vmem((2, groups, columns), F32),
        vmem((blocks, depth), F32),
        vmem((2, depth, LANE), F32),
        vmem((2, LANE, columns), F32),
        vmem((columns, LANE), F32),
        vmem((LANE, depth), F32),
        vmem((depth, 2 * LANE), BF16),
        vmem((LANE, depth), BF16),
        dma((2, blocks)),
        dma((blocks,)),
        dma((9,)),
        dma((HALVES,)), dma((HALVES,)), dma((HALVES,)), dma((HALVES,)),
        dma((units,)), dma((units,)), dma((units,)), dma((units,)),
        dma((HALVES,)), dma((HALVES,)), dma((HALVES,)), dma((HALVES,)),
    ]
    return kernel, scratch


def solution(mesh):
    n_wide, n_narrow = mesh.shape["wide"], mesh.shape["narrow"]

    def shards(tokens, gate_codes, up_codes, *rest):
        tok_rows = tokens.shape[0]
        depth, columns = gate_codes.shape
        kernel, scratch = make_kernel(n_wide, n_narrow, depth, columns, tok_rows)
        in_specs = [pl.BlockSpec(memory_space=pltpu.VMEM)] + [
            pl.BlockSpec(memory_space=pl.ANY)
        ] * 12
        return pl.pallas_call(
            kernel,
            out_shape=jax.ShapeDtypeStruct((tok_rows, depth), F32),
            in_specs=in_specs,
            out_specs=pl.BlockSpec(memory_space=pltpu.VMEM),
            scratch_shapes=scratch,
            compiler_params=pltpu.CompilerParams(
                collective_id=0, has_side_effects=True, vmem_limit_bytes=60 << 20
            ),
        )(tokens, gate_codes, up_codes, *rest)

    placed = (
        P("wide", "narrow"),
        P("narrow", "wide"),
        P("narrow", "wide"),
        P("narrow", "wide"),
        P("narrow", "wide"),
        P("wide", "narrow"),
        P("wide", "narrow"),
        P("narrow", None),
        P(None, "wide"),
        P("narrow", None),
        P(None, "wide"),
        P("wide", None),
        P(None, "narrow"),
    )
    return jax.shard_map(
        shards, mesh=mesh, in_specs=placed, out_specs=P("wide", "narrow"), check_vma=False
    )
```

time: 579 us -> 111 us (0.19)
  waiting for transfers between devices: 497 us -> 0 us
  Pallas kernels: 0 us -> 109 us
  matrix products: 34.5 us -> 0 us
  other arithmetic: 29.1 us -> 0 us
  between operations: 13.2 us -> 0.01 us
    psum x2 -> x0, waiting for transfers between devices: 406 us -> none  [the longest x1 293 us: shards(): summed = lax.psum(partial_rows, 'narrow')]
    pallas_call x0 -> x1, Pallas kernels: none -> 109 us  [shards(): pl.pallas_call(kernel, out_shape=jax.ShapeDtypeStruct((tok_rows, depth),...]
    reduce_scatter x1 -> x0, waiting for transfers between devices: 66.3 us -> none  [shards(): lax.psum_scatter(jnp.dot(hidden, down_w, preferred_element_type=jnp.float...]
    dot_general x6 -> x0, matrix products: 34.5 us -> none  [the longest x1 12.1 us: shards(): jnp.dot(lax.all_gather(tokens, 'wide', axis=0, tiled=True), both_w, prefe...]
    all_gather x1 -> x0, waiting for transfers between devices: 23.9 us -> none  [shards(): lax.all_gather(tokens, 'wide', axis=0, tiled=True)]
    unnamed x5 -> x0, other arithmetic: 14.3 us -> none
    convert_element_type x2 -> x0, other arithmetic: 9.09 us -> none  [the longest x1 8.22 us: dequant(): return values.reshape(rows, cols).astype(jnp.bfloat16)]
  transfers between devices with their start and end apart: 4 -> 0, of which waited for: 4 -> 0; matrix products, arithmetic and copies ran while one was open for 6% -> 0% of each run, Pallas kernels for 0% -> 0%
where the time goes in v1:
time: 111 us; the launch traced here: 110 us
  Pallas kernels  109 us (98%)
  local copies, waits for them, and re-layouts  1.67 us (2%)
    pallas_call x1, Pallas kernels, shards(): pl.pallas_call(kernel, out_shape=jax.ShapeDtypeStruct((tok_rows, depth),...  109 us

profile of v1, /device:TPU:1, one launch (start us, length us, event | category | flops | bytes accessed | tf_op | source)
XLA Modules:
  0.0 110.4 jit_solution(2951539145181710882)
XLA Ops:
  0.0 108.7 %shard_map.127 = f32[32,2048]{1,0:T(8,128)} custom-call(bf16[32,2048]{1,0:T(8,128)(2,1)} %tok.1, bf16[2048,1664]{1,0:T(8,128)(2,1)} %gate_codes.1, bf16[2048,1664]{1,0:T(8,128)(2,1)} %up_codes.1, f32[16,1664]{1,0:T(8,128)} %gate_scale.1, f32[16,1664]{1,0:T(8,128)} %up_scale.1, bf16[1664,2048]{1,0:T(8,128)(2,1)} %down_codes.1, f32[13,2048]{1,0:T(8,128)} %down_scale.1, ...), custom_call_target="tpu_custom_call" | custom-call | tf_op jit(solution)/shard_map/pallas_call | solution.py:338
  108.7 1.7 %copy.15 = f32[32,2048]{1,0:T(8,128)} copy(f32[32,2048]{1,0:T(8,128)} %shard_map.127) | data formatting | bytes 524288

commit v2 on v0

v2 whole, which is shorter than its diff:
```python
import jax
import jax.numpy as jnp
from jax import lax
from jax.experimental import pallas as pl
from jax.experimental.pallas import tpu as pltpu
from jax.sharding import PartitionSpec as P

MESH = pl.DeviceIdType.MESH
F32 = jnp.float32
BF16 = jnp.bfloat16
LANE = 128
HALVES = 2
CHUNKS = 4
UNITS = 7
X_FIRST = (1, 3, 5)
SKEW = (4, 8, 12, 16)


def remote(src, dst, send_sem, recv_sem, device):
    return pltpu.make_async_remote_copy(
        src_ref=src,
        dst_ref=dst,
        send_sem=send_sem,
        recv_sem=recv_sem,
        device_id=device,
        device_id_type=MESH,
    )


def aligned(value, size):
    return pl.multiple_of(value, size)


def make_kernel(n_wide, n_narrow, depth, columns, tok_rows):
    chips = n_wide // 2
    part = tok_rows // HALVES
    rows = chips * part
    ranks_x = n_narrow // 2
    own = rows // n_narrow
    groups = depth // LANE
    blocks = columns // LANE
    wide_k = depth + 2 * LANE
    block = 2 * LANE
    units = CHUNKS * UNITS
    last_block = (UNITS - 1) * block

    def kernel(
        tok, gate_codes, up_codes, gate_scale, up_scale, down_codes, down_scale,
        gate_left, gate_right, up_left, up_right, down_left, down_right,
        out,
        x_all, w_up, w_last, w_down, partial, land_1, land_2, half_sum, own_sum, hidden, acc,
        core_send, core_land, out_send, out_land,
        scale_v, dscale_v, left_v, right_v, dleft_v, dright_v, left_b, dright_b,
        load_w, load_d, load_s,
        tok_send, tok_recv, pair_send, pair_recv,
        ss_1, rs_1, ss_2, rs_2, hid_send, hid_recv_1, hid_recv_2,
        core_ss, core_rs, out_ss, out_rs,
    ):
        w = lax.axis_index("wide")
        n = lax.axis_index("narrow")
        chip, core = w // 2, lax.rem(w, 2)
        x, zh = n // 2, lax.rem(n, 2)
        sibling = (chip * 2 + (1 - core), n)
        z_peer = (w, x * 2 + (1 - zh))

        def wide_peer(d):
            return lax.rem(chip + d, chips)

        def x_peer(d):
            return lax.rem(x + d, ranks_x)

        small = [
            pltpu.make_async_copy(gate_left, left_v.at[0], load_s.at[0]),
            pltpu.make_async_copy(up_left, left_v.at[1], load_s.at[1]),
            pltpu.make_async_copy(gate_scale, scale_v.at[0], load_s.at[2]),
            pltpu.make_async_copy(up_scale, scale_v.at[1], load_s.at[3]),
            pltpu.make_async_copy(gate_right, right_v.at[0], load_s.at[4]),
            pltpu.make_async_copy(up_right, right_v.at[1], load_s.at[5]),
            pltpu.make_async_copy(down_scale, dscale_v, load_s.at[6]),
            pltpu.make_async_copy(down_left, dleft_v, load_s.at[7]),
            pltpu.make_async_copy(down_right, dright_v, load_s.at[8]),
        ]
        feats = pl.ds(0, depth)

        def cols_of(g, size=block):
            return pl.ds(aligned(g * block, size), size)

        def up_loads(g, target, size):
            return [
                pltpu.make_async_copy(
                    codes.at[:, cols_of(g, size)],
                    target.at[feats, pl.ds(i * size, size)],
                    load_w.at[i, g],
                )
                for i, codes in enumerate((gate_codes, up_codes))
            ]

        def down_load(g):
            here = pl.ds(aligned(g * LANE, LANE), LANE)
            return pltpu.make_async_copy(
                down_codes.at[here, :], w_down.at[here, feats], load_d.at[g]
            )

        with jax.named_scope("issue"):
            for copy in small[:6]:
                copy.start()

            @pl.loop(0, UNITS - 1)
            def _(g):
                for copy in up_loads(g, w_up.at[g], block):
                    copy.start()

            for copy in up_loads(UNITS - 1, w_last, LANE) + small[6:]:
                copy.start()

            @pl.loop(0, blocks)
            def _(g):
                down_load(g).start()

        with jax.named_scope("greet"):
            barrier = pltpu.get_barrier_semaphore()
            greet = [(wide_peer(d) * 2 + core, n) for d in range(1, chips)]
            greet += [(w, x_peer(d) * 2 + zh) for d in range(1, ranks_x)] + [z_peer, sibling]
            for device in greet:
                pl.semaphore_signal(barrier, inc=1, device_id=device, device_id_type=MESH)
            pl.semaphore_wait(barrier, len(greet))

        place = pl.ds(aligned(chip * part, part), part)

        def tokens_out(q):
            h, c = q // 2, q % 2

            @pl.when(core == c)
            def _():
                for d in range(1, chips):
                    remote(
                        tok.at[pl.ds(h * part, part), :],
                        x_all.at[q, place, feats],
                        tok_send.at[h],
                        tok_recv.at[h],
                        (wide_peer(d) * 2 + core, n),
                    ).start()
                x_all[q, place, feats] = tok[pl.ds(h * part, part), :]

        def pair_copy(q):
            both = x_all.at[q, :, feats]
            return remote(both, both, pair_send.at[q], pair_recv.at[q], sibling)

        def tokens_pair(q):
            h, c = q // 2, q % 2

            @pl.when(core == c)
            def _():
                got = x_all.at[q, pl.ds(0, (chips - 1) * part), feats]
                remote(got, got, tok_send.at[h], tok_recv.at[h], sibling).wait()
                pair_copy(q).start()

        def low_rank(q):
            @pl.when(core != q % 2)
            def _():
                pair_copy(q).wait_recv()

            x_all[q, :, pl.ds(depth, 2 * LANE)] = jnp.dot(
                x_all[q, :, feats], left_b[...], preferred_element_type=F32
            ).astype(BF16)

        def prepare():
            for copy in small[:6]:
                copy.wait()
            left_b[:, pl.ds(0, LANE)] = left_v[0].astype(BF16)
            left_b[:, pl.ds(LANE, LANE)] = left_v[1].astype(BF16)

            def widen(g, target, size):
                for copy in up_loads(g, target, size):
                    copy.wait()
                for i in range(2):
                    here = pl.ds(i * size, size)
                    for k in range(groups):
                        at = pl.ds(k * LANE, LANE)
                        scale = scale_v[i, pl.ds(k, 1), cols_of(g, size)]
                        target[at, here] = (target[at, here].astype(F32) * scale).astype(BF16)
                    right = right_v[i, :, cols_of(g, size)].astype(BF16)
                    target[pl.ds(depth + i * LANE, LANE), here] = right
                    target[pl.ds(depth + (1 - i) * LANE, LANE), here] = jnp.zeros_like(right)

            @pl.loop(0, UNITS - 1)
            def _(g):
                widen(g, w_up.at[g], block)

            widen(UNITS - 1, w_last, LANE)
            for copy in small[6:]:
                copy.wait()
            dright_b[...] = dright_v[...].astype(BF16)

            @pl.loop(0, blocks)
            def _(g):
                down_load(g).wait()
                here = pl.ds(aligned(g * LANE, LANE), LANE)
                scale = dscale_v[pl.ds(g, 1), :]
                w_down[here, feats] = (w_down[here, feats].astype(F32) * scale).astype(BF16)
                w_down[here, pl.ds(depth, LANE)] = dleft_v[here, :].astype(BF16)

        def variants(stage):
            def run(u):
                q, g = u // UNITS, lax.rem(u, UNITS)
                along_x = g == X_FIRST[0]
                for other in X_FIRST[1:]:
                    along_x = along_x | (g == other)
                narrow_block = g == UNITS - 1

                @pl.when(along_x)
                def _():
                    stage(u, q, g, True, block)

                @pl.when(jnp.logical_not(along_x | narrow_block))
                def _():
                    stage(u, q, g, False, block)

                @pl.when(narrow_block)
                def _():
                    stage(u, q, g, False, LANE)

            return run

        def start_of(x_first, xi, zi):
            return aligned(xi * 2 * own + zi * own if x_first else zi * ranks_x * own + xi * own, own)

        def bytes_of(buffer, u, count, size, send, recv):
            at = buffer.at[u, pl.ds(0, count), pl.ds(0, size)]
            return remote(at, at, send.at[u], recv.at[u], sibling)

        def wait_1(u, x_first, size):
            count = (ranks_x - 1) * 2 * own if x_first else ranks_x * own
            return bytes_of(land_1, u, count, size, ss_1, rs_1)

        def wait_2(u, x_first, size):
            count = own if x_first else (ranks_x - 1) * own
            return bytes_of(land_2, u, count, size, ss_2, rs_2)

        def first(u, q, g, x_first, size):
            cols = pl.ds(0, 2 * size)
            weights = w_up[g] if size == block else w_last[...]
            partial[u, :, cols] = jnp.dot(
                x_all[q], weights, preferred_element_type=F32
            ).astype(BF16)
            if x_first:
                for d in range(1, ranks_x):
                    xi = x_peer(d)
                    remote(
                        partial.at[u, pl.ds(start_of(True, xi, 0), 2 * own), cols],
                        land_1.at[u, pl.ds((d - 1) * 2 * own, 2 * own), cols],
                        ss_1.at[u],
                        rs_1.at[u],
                        (w, xi * 2 + zh),
                    ).start()
            else:
                remote(
                    partial.at[u, pl.ds(start_of(False, 0, 1 - zh), ranks_x * own), cols],
                    land_1.at[u, pl.ds(0, ranks_x * own), cols],
                    ss_1.at[u],
                    rs_1.at[u],
                    z_peer,
                ).start()

        def sum_1(u, q, g, x_first, size):
            cols = pl.ds(0, 2 * size)
            wait_1(u, x_first, 2 * size).wait_recv()
            if x_first:

                def total(zi):
                    value = partial[u, pl.ds(start_of(True, x, zi), own), cols].astype(F32)
                    for d in range(ranks_x - 1):
                        at = pl.ds(aligned(d * 2 * own + zi * own, own), own)
                        value = value + land_1[u, at, cols].astype(F32)
                    return value

                half_sum[u, pl.ds(0, own), cols] = total(1 - zh).astype(BF16)
                remote(
                    half_sum.at[u, pl.ds(0, own), cols],
                    land_2.at[u, pl.ds(0, own), cols],
                    ss_2.at[u],
                    rs_2.at[u],
                    z_peer,
                ).start()
                own_sum[u, :, cols] = total(zh)
            else:
                group = pl.ds(start_of(False, 0, zh), ranks_x * own)
                got = pl.ds(0, ranks_x * own)
                half_sum[u, got, cols] = (
                    partial[u, group, cols].astype(F32) + land_1[u, got, cols].astype(F32)
                ).astype(BF16)
                for d in range(1, ranks_x):
                    xi = x_peer(d)
                    remote(
                        half_sum.at[u, pl.ds(aligned(xi * own, own), own), cols],
                        land_2.at[u, pl.ds((d - 1) * own, own), cols],
                        ss_2.at[u],
                        rs_2.at[u],
                        (w, xi * 2 + zh),
                    ).start()
                mine = pl.ds(aligned(x * own, own), own)
                own_sum[u, :, cols] = (
                    partial[u, pl.ds(start_of(False, x, zh), own), cols].astype(F32)
                    + land_1[u, mine, cols].astype(F32)
                )

        def hidden_copy(u, at, size, recv, device):
            here = hidden.at[u, at, pl.ds(0, size)]
            return remote(here, here, hid_send.at[u], recv.at[u], device)

        def sum_2(u, q, g, x_first, size):
            wait_2(u, x_first, 2 * size).wait_recv()
            total = own_sum[u, :, pl.ds(0, 2 * size)]
            for d in range(1 if x_first else ranks_x - 1):
                total = total + land_2[u, pl.ds(d * own, own), pl.ds(0, 2 * size)].astype(F32)
            gate, up = total[:, :size], total[:, size:]
            mine = pl.ds(start_of(x_first, x, zh), own)
            hidden[u, mine, pl.ds(0, size)] = (gate / (1.0 + jnp.exp(-gate)) * up).astype(BF16)
            along_z = hid_recv_1 if x_first else hid_recv_2
            along_x = hid_recv_2 if x_first else hid_recv_1
            hidden_copy(u, mine, size, along_z, z_peer).start()
            for d in range(1, ranks_x):
                hidden_copy(u, mine, size, along_x, (w, x_peer(d) * 2 + zh)).start()

        def wait_early(u, x_first, size):
            count = own if x_first else (ranks_x - 1) * own
            return bytes_of(hidden, u, count, size, hid_send, hid_recv_1)

        def wait_late(u, x_first, size):
            count = (ranks_x - 1) * 2 * own if x_first else ranks_x * own
            return bytes_of(hidden, u, count, size, hid_send, hid_recv_2)

        def relay(u, q, g, x_first, size):
            wait_early(u, x_first, size).wait_recv()
            for d in range(1, ranks_x):
                xi = x_peer(d)
                if x_first:
                    at = pl.ds(start_of(True, x, 1 - zh), own)
                    device = (w, xi * 2 + zh)
                else:
                    at = pl.ds(start_of(False, xi, zh), own)
                    device = z_peer
                hidden_copy(u, at, size, hid_recv_2, device).start()

        def second(u, q, g, x_first, size):
            wait_late(u, x_first, size).wait_recv()
            acc[q] += jnp.dot(
                hidden[u, :, pl.ds(0, size)],
                w_down[cols_of(g, size), :],
                preferred_element_type=F32,
            )
            wait_1(u, x_first, 2 * size).wait_send()
            wait_2(u, x_first, 2 * size).wait_send()
            bytes_of(hidden, u, (n_narrow - 1) * own, size, hid_send, hid_recv_2).wait_send()

        def core_copy(h):
            return remote(core_send.at[h], core_land.at[h], core_ss.at[h], core_rs.at[h], sibling)

        def to_owning_core(q):
            low = acc[q, :, pl.ds(depth, LANE)].astype(BF16)
            acc[q, :, feats] += jnp.dot(low, dright_b[...], preferred_element_type=F32)

            @pl.when(core != q % 2)
            def _():
                core_send[q // 2] = acc[q, :, feats].astype(BF16)
                core_copy(q // 2).start()

        def to_owners(q):
            h = q // 2

            @pl.when(core == q % 2)
            def _():
                core_copy(h).wait_recv()
                both = acc[q, :, feats] + core_land[h].astype(F32)
                acc[q, :, feats] = both
                out_send[h] = both.astype(BF16)
                for d in range(1, chips):
                    peer = wide_peer(d)
                    remote(
                        out_send.at[h, pl.ds(aligned(peer * part, part), part)],
                        out_land.at[h, d - 1],
                        out_ss.at[h],
                        out_rs.at[h],
                        (peer * 2 + core, n),
                    ).start()

        def finish(q):
            h = q // 2

            @pl.when(core == q % 2)
            def _():
                remote(out_land.at[h], out_land.at[h], out_ss.at[h], out_rs.at[h], sibling).wait()
                total = acc[q, place, feats]
                for d in range(chips - 1):
                    total = total + out_land[h, d].astype(F32)
                out[pl.ds(h * part, part), :] = total
                pair_copy(q).wait_send()

            @pl.when(core != q % 2)
            def _():
                core_copy(h).wait_send()

        def scope(name, function, *given):
            with jax.named_scope(name):
                function(*given)

        scope("tokens_out", tokens_out, 0)
        acc[...] = jnp.zeros_like(acc)
        scope("prepare", prepare)
        scope("tokens_out", tokens_out, 1)
        scope("tokens_pair", tokens_pair, 0)
        scope("low_rank", low_rank, 0)

        events = {}
        for q in range(1, CHUNKS):
            if q > 1:
                events.setdefault(UNITS * (q - 2) + 1, []).append(("tokens_out", tokens_out, q))
            events.setdefault(UNITS * q - 4, []).append(("tokens_pair", tokens_pair, q))
            events.setdefault(UNITS * q - 1, []).append(("low_rank", low_rank, q))
        for q in range(CHUNKS - 1):
            done = UNITS * (q + 1) - 1 + SKEW[3]
            events.setdefault(done, []).append(("to_owning_core", to_owning_core, q))
            events.setdefault(done + 2, []).append(("to_owners", to_owners, q))
        stages = [("first", 0, variants(first))]
        for name, skew, stage in zip(
            ("sum_1", "sum_2", "relay", "second"), SKEW, (sum_1, sum_2, relay, second)
        ):
            stages.append((name, skew, variants(stage)))

        @pl.loop(0, units + SKEW[3])
        def _(t):
            for name, skew, stage in stages:

                @pl.when((t >= skew) & (t < units + skew))
                def _():
                    scope(name, stage, t - skew)

            for at, todo in events.items():

                @pl.when(t == at)
                def _():
                    for name, function, q in todo:
                        scope(name, function, q)

        scope("to_owning_core", to_owning_core, CHUNKS - 1)
        for q in range(CHUNKS - 2):
            scope("finish", finish, q)
        scope("to_owners", to_owners, CHUNKS - 1)
        for q in range(CHUNKS - 2, CHUNKS):
            scope("finish", finish, q)

    vmem = pltpu.VMEM
    dma = pltpu.SemaphoreType.DMA
    scratch = [
        vmem((CHUNKS, rows, wide_k), BF16),
        vmem((UNITS - 1, wide_k, 2 * block), BF16),
        vmem((wide_k, block), BF16),
        vmem((columns, depth + LANE), BF16),
        vmem((units, rows, 2 * block), BF16),
        vmem((units, (ranks_x - 1) * 2 * own, 2 * block), BF16),
        vmem((units, (ranks_x - 1) * own, 2 * block), BF16),
        vmem((units, ranks_x * own, 2 * block), BF16),
        vmem((units, own, 2 * block), F32),
        vmem((units, rows, block), BF16),
        vmem((CHUNKS, rows, depth + LANE), F32),
        vmem((HALVES, rows, depth), BF16),
        vmem((HALVES, rows, depth), BF16),
        vmem((HALVES, rows, depth), BF16),
        vmem((HALVES, chips - 1, part, depth), BF16),
        vmem((2, groups, columns), F32),
        vmem((blocks, depth), F32),
        vmem((2, depth, LANE), F32),
        vmem((2, LANE, columns), F32),
        vmem((columns, LANE), F32),
        vmem((LANE, depth), F32),
        vmem((depth, 2 * LANE), BF16),
        vmem((LANE, depth), BF16),
        dma((2, UNITS)),
        dma((blocks,)),
        dma((9,)),
        dma((HALVES,)), dma((HALVES,)), dma((CHUNKS,)), dma((CHUNKS,)),
        dma((units,)), dma((units,)), dma((units,)), dma((units,)),
        dma((units,)), dma((units,)), dma((units,)),
        dma((HALVES,)), dma((HALVES,)), dma((HALVES,)), dma((HALVES,)),
    ]
    return kernel, scratch


def solution(mesh):
    n_wide, n_narrow = mesh.shape["wide"], mesh.shape["narrow"]

    def shards(tokens, gate_codes, up_codes, *rest):
        tok_rows = tokens.shape[0]
        depth, columns = gate_codes.shape
        kernel, scratch = make_kernel(n_wide, n_narrow, depth, columns, tok_rows)
        in_specs = [pl.BlockSpec(memory_space=pltpu.VMEM)] + [
            pl.BlockSpec(memory_space=pl.ANY)
        ] * 12
        return pl.pallas_call(
            kernel,
            out_shape=jax.ShapeDtypeStruct((tok_rows, depth), F32),
            in_specs=in_specs,
            out_specs=pl.BlockSpec(memory_space=pltpu.VMEM),
            scratch_shapes=scratch,
            compiler_params=pltpu.CompilerParams(
                collective_id=0, has_side_effects=True, vmem_limit_bytes=60 << 20
            ),
        )(tokens, gate_codes, up_codes, *rest)

    placed = (
        P("wide", "narrow"),
        P("narrow", "wide"),
        P("narrow", "wide"),
        P("narrow", "wide"),
        P("narrow", "wide"),
        P("wide", "narrow"),
        P("wide", "narrow"),
        P("narrow", None),
        P(None, "wide"),
        P("narrow", None),
        P(None, "wide"),
        P("wide", None),
        P(None, "narrow"),
    )
    return jax.shard_map(
        shards, mesh=mesh, in_specs=placed, out_specs=P("wide", "narrow"), check_vma=False
    )
```

time: 579 us -> 91.4 us (0.16)
  waiting for transfers between devices: 497 us -> 0 us
  Pallas kernels: 0 us -> 89.6 us
  matrix products: 34.5 us -> 0 us
  other arithmetic: 29.1 us -> 0 us
  between operations: 13.2 us -> 0.01 us
    psum x2 -> x0, waiting for transfers between devices: 406 us -> none  [the longest x1 293 us: shards(): summed = lax.psum(partial_rows, 'narrow')]
    pallas_call x0 -> x1, Pallas kernels: none -> 89.6 us  [shards(): pl.pallas_call(kernel, out_shape=jax.ShapeDtypeStruct((tok_rows, depth),...]
    reduce_scatter x1 -> x0, waiting for transfers between devices: 66.3 us -> none  [shards(): lax.psum_scatter(jnp.dot(hidden, down_w, preferred_element_type=jnp.float...]
    dot_general x6 -> x0, matrix products: 34.5 us -> none  [the longest x1 12.1 us: shards(): jnp.dot(lax.all_gather(tokens, 'wide', axis=0, tiled=True), both_w, prefe...]
    all_gather x1 -> x0, waiting for transfers between devices: 23.9 us -> none  [shards(): lax.all_gather(tokens, 'wide', axis=0, tiled=True)]
    unnamed x5 -> x0, other arithmetic: 14.3 us -> none
    convert_element_type x2 -> x0, other arithmetic: 9.09 us -> none  [the longest x1 8.22 us: dequant(): return values.reshape(rows, cols).astype(jnp.bfloat16)]
  transfers between devices with their start and end apart: 4 -> 0, of which waited for: 4 -> 0; matrix products, arithmetic and copies ran while one was open for 6% -> 0% of each run, Pallas kernels for 0% -> 0%
where the time goes in v2:
time: 91.4 us; the launch traced here: 91.2 us
  Pallas kernels  89.6 us (98%)
  local copies, waits for them, and re-layouts  1.67 us (2%)
    pallas_call x1, Pallas kernels, shards(): pl.pallas_call(kernel, out_shape=jax.ShapeDtypeStruct((tok_rows, depth),...  89.6 us

profile of v2, /device:TPU:1, one launch (start us, length us, event | category | flops | bytes accessed | tf_op | source)
XLA Modules:
  0.0 91.2 jit_solution(17680073101333864411)
XLA Ops:
  0.0 89.6 %shard_map.127 = f32[32,2048]{1,0:T(8,128)} custom-call(bf16[32,2048]{1,0:T(8,128)(2,1)} %tok.1, bf16[2048,1664]{1,0:T(8,128)(2,1)} %gate_codes.1, bf16[2048,1664]{1,0:T(8,128)(2,1)} %up_codes.1, f32[16,1664]{1,0:T(8,128)} %gate_scale.1, f32[16,1664]{1,0:T(8,128)} %up_scale.1, bf16[1664,2048]{1,0:T(8,128)(2,1)} %down_codes.1, f32[13,2048]{1,0:T(8,128)} %down_scale.1, ...), custom_call_target="tpu_custom_call" | custom-call | tf_op jit(solution)/shard_map/pallas_call | solution.py:499
  89.6 1.7 %copy.15 = f32[32,2048]{1,0:T(8,128)} copy(f32[32,2048]{1,0:T(8,128)} %shard_map.127) | data formatting | bytes 524288

commit v3 on v2

--- a/solution.py
+++ b/solution.py
@@ -14,6 +14,11 @@
 UNITS = 7
 X_FIRST = (1, 3, 5)
 SKEW = (4, 8, 12, 16)
+AFTER = (3, 9)
+OUT_AT = (-1, 0, 3)
+RELAY_AT = (-1, 4, 10)
+PAIR_AT = (1, 9, 16)
+SPREAD = 3
 
 
 def remote(src, dst, send_sem, recv_sem, device):
@@ -33,6 +38,7 @@
 
 def make_kernel(n_wide, n_narrow, depth, columns, tok_rows):
     chips = n_wide // 2
+    ranks_y = chips // 2
     part = tok_rows // HALVES
     rows = chips * part
     ranks_x = n_narrow // 2
@@ -49,22 +55,28 @@
         gate_left, gate_right, up_left, up_right, down_left, down_right,
         out,
         x_all, w_up, w_last, w_down, partial, land_1, land_2, half_sum, own_sum, hidden, acc,
-        core_send, core_land, out_send, out_land,
+        core_send, core_land, out_send, out_land, z_send, z_land,
         scale_v, dscale_v, left_v, right_v, dleft_v, dright_v, left_b, dright_b,
         load_w, load_d, load_s,
-        tok_send, tok_recv, pair_send, pair_recv,
+        tok_send, tok_first, tok_recv, tok_recv_z, pair_send, pair_recv,
         ss_1, rs_1, ss_2, rs_2, hid_send, hid_recv_1, hid_recv_2,
-        core_ss, core_rs, out_ss, out_rs,
+        core_ss, core_rs, out_ss, out_rs, z_ss, z_rs,
     ):
         w = lax.axis_index("wide")
         n = lax.axis_index("narrow")
-        chip, core = w // 2, lax.rem(w, 2)
+        core, y, zl = lax.rem(w, 2), lax.rem(w // 2, ranks_y), w // chips
         x, zh = n // 2, lax.rem(n, 2)
-        sibling = (chip * 2 + (1 - core), n)
+        sibling = (w + 1 - 2 * core, n)
         z_peer = (w, x * 2 + (1 - zh))
 
-        def wide_peer(d):
-            return lax.rem(chip + d, chips)
+        def y_peer(d):
+            return lax.rem(y + d, ranks_y)
+
+        def chip_at(yi, zi):
+            return (zi * chips + yi * 2 + core, n)
+
+        def tok_place(yi, zi, count=1):
+            return pl.ds(aligned((yi * 2 + zi) * part, part), count * part)
 
         def x_peer(d):
             return lax.rem(x + d, ranks_x)
@@ -119,41 +131,75 @@
 
         with jax.named_scope("greet"):
             barrier = pltpu.get_barrier_semaphore()
-            greet = [(wide_peer(d) * 2 + core, n) for d in range(1, chips)]
-            greet += [(w, x_peer(d) * 2 + zh) for d in range(1, ranks_x)] + [z_peer, sibling]
+            greet = [chip_at(y_peer(d), zi) for d in range(1, ranks_y) for zi in range(2)]
+            greet += [chip_at(y, 1 - zl)]
+            greet += [(w, x_peer(d) * 2 + zi) for d in range(1, ranks_x) for zi in range(2)]
+            greet += [z_peer, sibling]
             for device in greet:
                 pl.semaphore_signal(barrier, inc=1, device_id=device, device_id_type=MESH)
             pl.semaphore_wait(barrier, len(greet))
 
-        place = pl.ds(aligned(chip * part, part), part)
+        place = tok_place(y, zl)
 
         def tokens_out(q):
             h, c = q // 2, q % 2
 
             @pl.when(core == c)
             def _():
-                for d in range(1, chips):
+                def send(recv, device):
                     remote(
                         tok.at[pl.ds(h * part, part), :],
                         x_all.at[q, place, feats],
                         tok_send.at[h],
-                        tok_recv.at[h],
-                        (wide_peer(d) * 2 + core, n),
+                        recv,
+                        device,
                     ).start()
+
+                send(tok_first.at[0] if q == 0 else tok_recv_z.at[h], chip_at(y, 1 - zl))
+                for d in range(1, ranks_y):
+                    send(tok_first.at[d] if q == 0 else tok_recv.at[h], chip_at(y_peer(d), zl))
+                    if q == 0:
+                        send(tok_first.at[ranks_y - 1 + d], chip_at(y_peer(d), 1 - zl))
                 x_all[q, place, feats] = tok[pl.ds(h * part, part), :]
+
+        def tokens_got(q, count, recv):
+            got = x_all.at[q, pl.ds(0, count * part), feats]
+            return remote(got, got, tok_send.at[q // 2], recv.at[q // 2], sibling)
+
+        def tokens_relay(q):
+            @pl.when(core == q % 2)
+            def _():
+                tokens_got(q, 1, tok_recv_z).wait_recv()
+                here = x_all.at[q, tok_place(y, 1 - zl), feats]
+                for d in range(1, ranks_y):
+                    remote(
+                        here, here, tok_send.at[q // 2], tok_recv.at[q // 2], chip_at(y_peer(d), zl)
+                    ).start()
 
         def pair_copy(q):
             both = x_all.at[q, :, feats]
             return remote(both, both, pair_send.at[q], pair_recv.at[q], sibling)
 
+        def pass_on(at):
+            here = x_all.at[0, at, feats]
+            remote(here, here, pair_send.at[0], pair_recv.at[0], sibling).start()
+
         def tokens_pair(q):
-            h, c = q // 2, q % 2
-
-            @pl.when(core == c)
-            def _():
-                got = x_all.at[q, pl.ds(0, (chips - 1) * part), feats]
-                remote(got, got, tok_send.at[h], tok_recv.at[h], sibling).wait()
-                pair_copy(q).start()
+            @pl.when(core == q % 2)
+            def _():
+                if q > 0:
+                    tokens_got(q, chips - 2, tok_recv).wait_recv()
+                    pair_copy(q).start()
+                else:
+                    pass_on(place)
+                    for d in (0, 1, 3, 4, 6, 2, 5):
+                        side = 0 if d == 0 else (d - 1) % (ranks_y - 1) + 1
+                        yi = lax.rem(y + ranks_y - side, ranks_y)
+                        here = tok_place(yi, zl if 0 < d < ranks_y else 1 - zl)
+                        got = x_all.at[q, here, feats]
+                        remote(got, got, tok_send.at[0], tok_first.at[d], sibling).wait_recv()
+                        pass_on(here)
+                tokens_got(q, chips - 1, tok_recv).wait_send()
 
         def low_rank(q):
             @pl.when(core != q % 2)
@@ -200,27 +246,8 @@
                 w_down[here, feats] = (w_down[here, feats].astype(F32) * scale).astype(BF16)
                 w_down[here, pl.ds(depth, LANE)] = dleft_v[here, :].astype(BF16)
 
-        def variants(stage):
-            def run(u):
-                q, g = u // UNITS, lax.rem(u, UNITS)
-                along_x = g == X_FIRST[0]
-                for other in X_FIRST[1:]:
-                    along_x = along_x | (g == other)
-                narrow_block = g == UNITS - 1
-
-                @pl.when(along_x)
-                def _():
-                    stage(u, q, g, True, block)
-
-                @pl.when(jnp.logical_not(along_x | narrow_block))
-                def _():
-                    stage(u, q, g, False, block)
-
-                @pl.when(narrow_block)
-                def _():
-                    stage(u, q, g, False, LANE)
-
-            return run
+        def run(stage, q, g):
+            stage(q * UNITS + g, q, g, g in X_FIRST, LANE if g == UNITS - 1 else block)
 
         def start_of(x_first, xi, zi):
             return aligned(xi * 2 * own + zi * own if x_first else zi * ranks_x * own + xi * own, own)
@@ -261,6 +288,27 @@
                     rs_1.at[u],
                     z_peer,
                 ).start()
+
+        def hidden_copy(u, at, size, recv, device):
+            here = hidden.at[u, at, pl.ds(0, size)]
+            return remote(here, here, hid_send.at[u], recv.at[u], device)
+
+        def activate(u, q, total, x_first, size):
+            gate, up = total[:, :size], total[:, size:]
+            mine = pl.ds(start_of(x_first, x, zh), own)
+            hidden[u, mine, pl.ds(0, size)] = (gate / (1.0 + jnp.exp(-gate)) * up).astype(BF16)
+            along_z = hid_recv_1 if x_first else hid_recv_2
+            along_x = hid_recv_2 if x_first else hid_recv_1
+            hidden_copy(u, mine, size, along_z, z_peer).start()
+            for d in range(1, ranks_x):
+                xi = x_peer(d) * 2
+                hidden_copy(u, mine, size, along_x, (w, xi + zh)).start()
+
+            @pl.when(q >= SPREAD)
+            def _():
+                for d in range(1, ranks_x):
+                    device = (w, x_peer(d) * 2 + 1 - zh)
+                    hidden_copy(u, mine, size, hid_recv_2, device).start()
 
         def sum_1(u, q, g, x_first, size):
             cols = pl.ds(0, 2 * size)
@@ -304,23 +352,12 @@
                     + land_1[u, mine, cols].astype(F32)
                 )
 
-        def hidden_copy(u, at, size, recv, device):
-            here = hidden.at[u, at, pl.ds(0, size)]
-            return remote(here, here, hid_send.at[u], recv.at[u], device)
-
         def sum_2(u, q, g, x_first, size):
             wait_2(u, x_first, 2 * size).wait_recv()
             total = own_sum[u, :, pl.ds(0, 2 * size)]
             for d in range(1 if x_first else ranks_x - 1):
                 total = total + land_2[u, pl.ds(d * own, own), pl.ds(0, 2 * size)].astype(F32)
-            gate, up = total[:, :size], total[:, size:]
-            mine = pl.ds(start_of(x_first, x, zh), own)
-            hidden[u, mine, pl.ds(0, size)] = (gate / (1.0 + jnp.exp(-gate)) * up).astype(BF16)
-            along_z = hid_recv_1 if x_first else hid_recv_2
-            along_x = hid_recv_2 if x_first else hid_recv_1
-            hidden_copy(u, mine, size, along_z, z_peer).start()
-            for d in range(1, ranks_x):
-                hidden_copy(u, mine, size, along_x, (w, x_peer(d) * 2 + zh)).start()
+            activate(u, q, total, x_first, size)
 
         def wait_early(u, x_first, size):
             count = own if x_first else (ranks_x - 1) * own
@@ -332,15 +369,18 @@
 
         def relay(u, q, g, x_first, size):
             wait_early(u, x_first, size).wait_recv()
-            for d in range(1, ranks_x):
-                xi = x_peer(d)
-                if x_first:
-                    at = pl.ds(start_of(True, x, 1 - zh), own)
-                    device = (w, xi * 2 + zh)
-                else:
-                    at = pl.ds(start_of(False, xi, zh), own)
-                    device = z_peer
-                hidden_copy(u, at, size, hid_recv_2, device).start()
+
+            @pl.when(q < SPREAD)
+            def _():
+                for d in range(1, ranks_x):
+                    xi = x_peer(d)
+                    if x_first:
+                        at = pl.ds(start_of(True, x, 1 - zh), own)
+                        device = (w, xi * 2 + zh)
+                    else:
+                        at = pl.ds(start_of(False, xi, zh), own)
+                        device = z_peer
+                    hidden_copy(u, at, size, hid_recv_2, device).start()
 
         def second(u, q, g, x_first, size):
             wait_late(u, x_first, size).wait_recv()
@@ -365,6 +405,9 @@
                 core_send[q // 2] = acc[q, :, feats].astype(BF16)
                 core_copy(q // 2).start()
 
+        def out_copy(h, src, dst, send, recv, device):
+            return remote(src, dst, send.at[h], recv.at[h], device)
+
         def to_owners(q):
             h = q // 2
 
@@ -374,26 +417,73 @@
                 both = acc[q, :, feats] + core_land[h].astype(F32)
                 acc[q, :, feats] = both
                 out_send[h] = both.astype(BF16)
-                for d in range(1, chips):
-                    peer = wide_peer(d)
+                for d in range(1, ranks_y):
+                    yi = y_peer(d)
+                    if q < CHUNKS - 1:
+                        at = pl.ds((d - 1) * 2 * part, 2 * part)
+                        remote(
+                            out_send.at[h, tok_place(yi, 0, 2)],
+                            out_land.at[h, at],
+                            out_ss.at[h],
+                            out_rs.at[h],
+                            chip_at(yi, zl),
+                        ).start()
+                        continue
+                    for zi in range(2):
+                        at = pl.ds(aligned(((d - 1) * 2 + zl) * part, part), part)
+                        remote(
+                            out_send.at[h, tok_place(yi, zi)],
+                            out_land.at[h, at],
+                            out_ss.at[h],
+                            out_rs.at[h],
+                            chip_at(yi, zi),
+                        ).start()
+                if q == CHUNKS - 1:
                     remote(
-                        out_send.at[h, pl.ds(aligned(peer * part, part), part)],
-                        out_land.at[h, d - 1],
-                        out_ss.at[h],
-                        out_rs.at[h],
-                        (peer * 2 + core, n),
+                        out_send.at[h, tok_place(y, 1 - zl)],
+                        z_land.at[h],
+                        z_ss.at[h],
+                        z_rs.at[h],
+                        chip_at(y, 1 - zl),
                     ).start()
+
+        def out_wait(h):
+            got = out_land.at[h]
+            return remote(got, got, out_ss.at[h], out_rs.at[h], sibling)
+
+        def z_copy(h):
+            return remote(z_send.at[h], z_land.at[h], z_ss.at[h], z_rs.at[h], chip_at(y, 1 - zl))
+
+        def to_z(q):
+            h = q // 2
+
+            @pl.when(core == q % 2)
+            def _():
+                out_wait(h).wait()
+
+                def total(zi):
+                    value = acc[q, tok_place(y, zi), feats]
+                    for d in range(ranks_y - 1):
+                        at = pl.ds(aligned((d * 2 + zi) * part, part), part)
+                        value = value + out_land[h, at].astype(F32)
+                    return value
+
+                z_send[h] = total(1 - zl).astype(BF16)
+                z_copy(h).start()
+                acc[q, place, feats] = total(zl)
 
         def finish(q):
             h = q // 2
 
             @pl.when(core == q % 2)
             def _():
-                remote(out_land.at[h], out_land.at[h], out_ss.at[h], out_rs.at[h], sibling).wait()
                 total = acc[q, place, feats]
-                for d in range(chips - 1):
-                    total = total + out_land[h, d].astype(F32)
-                out[pl.ds(h * part, part), :] = total
+                if q == CHUNKS - 1:
+                    out_wait(h).wait()
+                    for d in range((ranks_y - 1) * 2):
+                        total = total + out_land[h, pl.ds(d * part, part)].astype(F32)
+                z_copy(h).wait()
+                out[pl.ds(h * part, part), :] = total + z_land[h].astype(F32)
                 pair_copy(q).wait_send()
 
             @pl.when(core != q % 2)
@@ -407,46 +497,60 @@
         scope("tokens_out", tokens_out, 0)
         acc[...] = jnp.zeros_like(acc)
         scope("prepare", prepare)
-        scope("tokens_out", tokens_out, 1)
+        if OUT_AT[0] < 0:
+            scope("tokens_out", tokens_out, 1)
         scope("tokens_pair", tokens_pair, 0)
+        if RELAY_AT[0] < 0:
+            scope("tokens_relay", tokens_relay, 1)
         scope("low_rank", low_rank, 0)
 
         events = {}
         for q in range(1, CHUNKS):
-            if q > 1:
-                events.setdefault(UNITS * (q - 2) + 1, []).append(("tokens_out", tokens_out, q))
-            events.setdefault(UNITS * q - 4, []).append(("tokens_pair", tokens_pair, q))
+            if OUT_AT[q - 1] >= 0:
+                events.setdefault(OUT_AT[q - 1], []).append(("tokens_out", tokens_out, q))
+            if RELAY_AT[q - 1] >= 0:
+                events.setdefault(RELAY_AT[q - 1], []).append(("tokens_relay", tokens_relay, q))
+            events.setdefault(PAIR_AT[q - 1], []).append(("tokens_pair", tokens_pair, q))
             events.setdefault(UNITS * q - 1, []).append(("low_rank", low_rank, q))
         for q in range(CHUNKS - 1):
             done = UNITS * (q + 1) - 1 + SKEW[3]
             events.setdefault(done, []).append(("to_owning_core", to_owning_core, q))
-            events.setdefault(done + 2, []).append(("to_owners", to_owners, q))
-        stages = [("first", 0, variants(first))]
-        for name, skew, stage in zip(
-            ("sum_1", "sum_2", "relay", "second"), SKEW, (sum_1, sum_2, relay, second)
-        ):
-            stages.append((name, skew, variants(stage)))
-
-        @pl.loop(0, units + SKEW[3])
-        def _(t):
-            for name, skew, stage in stages:
-
-                @pl.when((t >= skew) & (t < units + skew))
-                def _():
-                    scope(name, stage, t - skew)
-
-            for at, todo in events.items():
-
-                @pl.when(t == at)
-                def _():
-                    for name, function, q in todo:
-                        scope(name, function, q)
-
-        scope("to_owning_core", to_owning_core, CHUNKS - 1)
-        for q in range(CHUNKS - 2):
-            scope("finish", finish, q)
-        scope("to_owners", to_owners, CHUNKS - 1)
-        for q in range(CHUNKS - 2, CHUNKS):
+            events.setdefault(done + AFTER[0], []).append(("to_owners", to_owners, q))
+            events.setdefault(done + AFTER[1], []).append(("to_z", to_z, q))
+        stages = [("first", 0, first), ("sum_1", SKEW[0], sum_1), ("sum_2", SKEW[1], sum_2)]
+        stages += [("relay", SKEW[2], relay), ("second", SKEW[3], second)]
+        steps = units + SKEW[3]
+        late = [item for at, todo in sorted(events.items()) if at >= steps for item in todo]
+
+        @pl.loop(0, (steps + UNITS - 1) // UNITS)
+        def _(turn):
+            for step in range(UNITS):
+                for name, skew, stage in stages:
+                    back, g = divmod(step - skew, UNITS)
+
+                    @pl.when((turn + back >= 0) & (turn + back < CHUNKS))
+                    def _():
+                        scope(name, run, stage, turn + back, g)
+
+                for at, todo in sorted(events.items()):
+                    if at % UNITS != step or at >= steps:
+                        continue
+
+                    @pl.when(turn == at // UNITS)
+                    def _():
+                        for name, function, q in todo:
+                            scope(name, function, q)
+
+        last = CHUNKS - 1
+        scope("to_owning_core", to_owning_core, last)
+        for name, function, q in late:
+            if q % 2 != last % 2:
+                scope(name, function, q)
+        scope("to_owners", to_owners, last)
+        for name, function, q in late:
+            if q % 2 == last % 2:
+                scope(name, function, q)
+        for q in range(CHUNKS):
             scope("finish", finish, q)
 
     vmem = pltpu.VMEM
@@ -466,7 +570,9 @@
         vmem((HALVES, rows, depth), BF16),
         vmem((HALVES, rows, depth), BF16),
         vmem((HALVES, rows, depth), BF16),
-        vmem((HALVES, chips - 1, part, depth), BF16),
+        vmem((HALVES, (ranks_y - 1) * 2 * part, depth), BF16),
+        vmem((HALVES, part, depth), BF16),
+        vmem((HALVES, part, depth), BF16),
         vmem((2, groups, columns), F32),
         vmem((blocks, depth), F32),
         vmem((2, depth, LANE), F32),
@@ -478,10 +584,11 @@
         dma((2, UNITS)),
         dma((blocks,)),
         dma((9,)),
-        dma((HALVES,)), dma((HALVES,)), dma((CHUNKS,)), dma((CHUNKS,)),
+        dma((HALVES,)), dma((chips - 1,)), dma((HALVES,)), dma((HALVES,)), dma((CHUNKS,)), dma((CHUNKS,)),
         dma((units,)), dma((units,)), dma((units,)), dma((units,)),
         dma((units,)), dma((units,)), dma((units,)),
         dma((HALVES,)), dma((HALVES,)), dma((HALVES,)), dma((HALVES,)),
+        dma((HALVES,)), dma((HALVES,)),
     ]
     return kernel, scratch
 

time: 91.4 us -> 79.7 us (0.87)
  Pallas kernels: 89.6 us -> 77.8 us
    pallas_call x1, Pallas kernels: 89.6 us -> 77.8 us  [shards(): pl.pallas_call(kernel, out_shape=jax.ShapeDtypeStruct((tok_rows, depth),...]
where the time goes in v3:
time: 79.7 us; the launch traced here: 79.5 us
  Pallas kernels  77.8 us (98%)
  local copies, waits for them, and re-layouts  1.67 us (2%)
    pallas_call x1, Pallas kernels, shards(): pl.pallas_call(kernel, out_shape=jax.ShapeDtypeStruct((tok_rows, depth),...  77.8 us
    unnamed x1, local copies, waits for them, and re-layouts  1.67 us

profile of v3, /device:TPU:1, one launch (start us, length us, event | category | flops | bytes accessed | tf_op | source)
XLA Modules:
  0.0 79.5 jit_solution(8089149250942119073)
XLA Ops:
  0.0 77.8 %shard_map.127 = f32[32,2048]{1,0:T(8,128)} custom-call(bf16[32,2048]{1,0:T(8,128)(2,1)} %tok.1, bf16[2048,1664]{1,0:T(8,128)(2,1)} %gate_codes.1, bf16[2048,1664]{1,0:T(8,128)(2,1)} %up_codes.1, f32[16,1664]{1,0:T(8,128)} %gate_scale.1, f32[16,1664]{1,0:T(8,128)} %up_scale.1, bf16[1664,2048]{1,0:T(8,128)(2,1)} %down_codes.1, f32[13,2048]{1,0:T(8,128)} %down_scale.1, ...), custom_call_target="tpu_custom_call" | custom-call | tf_op jit(solution)/shard_map/pallas_call | solution.py:606
  77.8 1.7 %copy.15 = f32[32,2048]{1,0:T(8,128)} copy(f32[32,2048]{1,0:T(8,128)} %shard_map.127) | data formatting | bytes 524288

commit v4 on v3

--- a/solution.py
+++ b/solution.py
@@ -18,6 +18,9 @@
 OUT_AT = (-1, 0, 3)
 RELAY_AT = (-1, 4, 10)
 PAIR_AT = (1, 9, 16)
+PIECES = 2
+FAR_FIRST = (2, 1, 3)
+DIRECT = (4, 5, 6)
 SPREAD = 3
 
 
@@ -61,6 +64,7 @@
         tok_send, tok_first, tok_recv, tok_recv_z, pair_send, pair_recv,
         ss_1, rs_1, ss_2, rs_2, hid_send, hid_recv_1, hid_recv_2,
         core_ss, core_rs, out_ss, out_rs, z_ss, z_rs,
+        piece_cs, piece_cr, piece_os, piece_or, piece_zs, piece_zr,
     ):
         w = lax.axis_index("wide")
         n = lax.axis_index("narrow")
@@ -264,30 +268,64 @@
             count = own if x_first else (ranks_x - 1) * own
             return bytes_of(land_2, u, count, size, ss_2, rs_2)
 
+        def in_two_ways(q, g, straight, stepwise):
+            if g not in DIRECT:
+                stepwise()
+                return
+            pl.when(q == CHUNKS - 1)(straight)
+            pl.when(q < CHUNKS - 1)(stepwise)
+
+        def slots(u, x_first, cols):
+            for d in range(ranks_x):
+                for dz in range(2):
+                    if d == 0 and dz == 0:
+                        continue
+                    if x_first:
+                        one, at = d > 0, (d - 1) * 2 + dz if d > 0 else 0
+                    else:
+                        one, at = dz == 1, d if dz == 1 else d - 1
+                    here = pl.ds(at * own, own)
+                    yield d, dz, one, (land_1 if one else land_2).at[u, here, cols]
+
         def first(u, q, g, x_first, size):
             cols = pl.ds(0, 2 * size)
             weights = w_up[g] if size == block else w_last[...]
             partial[u, :, cols] = jnp.dot(
                 x_all[q], weights, preferred_element_type=F32
             ).astype(BF16)
-            if x_first:
-                for d in range(1, ranks_x):
+            def straight():
+                for d, dz, one, land in slots(u, x_first, cols):
                     xi = x_peer(d)
+                    zi = 1 - zh if dz else zh
                     remote(
-                        partial.at[u, pl.ds(start_of(True, xi, 0), 2 * own), cols],
-                        land_1.at[u, pl.ds((d - 1) * 2 * own, 2 * own), cols],
+                        partial.at[u, pl.ds(start_of(x_first, xi, zi), own), cols],
+                        land,
+                        (ss_1 if one else ss_2).at[u],
+                        (rs_1 if one else rs_2).at[u],
+                        (w, xi * 2 + zi),
+                    ).start()
+
+            def stepwise():
+                if x_first:
+                    for d in range(1, ranks_x):
+                        xi = x_peer(d)
+                        remote(
+                            partial.at[u, pl.ds(start_of(True, xi, 0), 2 * own), cols],
+                            land_1.at[u, pl.ds((d - 1) * 2 * own, 2 * own), cols],
+                            ss_1.at[u],
+                            rs_1.at[u],
+                            (w, xi * 2 + zh),
+                        ).start()
+                else:
+                    remote(
+                        partial.at[u, pl.ds(start_of(False, 0, 1 - zh), ranks_x * own), cols],
+                        land_1.at[u, pl.ds(0, ranks_x * own), cols],
                         ss_1.at[u],
                         rs_1.at[u],
-                        (w, xi * 2 + zh),
+                        z_peer,
                     ).start()
-            else:
-                remote(
-                    partial.at[u, pl.ds(start_of(False, 0, 1 - zh), ranks_x * own), cols],
-                    land_1.at[u, pl.ds(0, ranks_x * own), cols],
-                    ss_1.at[u],
-                    rs_1.at[u],
-                    z_peer,
-                ).start()
+
+            in_two_ways(q, g, straight, stepwise)
 
         def hidden_copy(u, at, size, recv, device):
             here = hidden.at[u, at, pl.ds(0, size)]
@@ -313,51 +351,65 @@
         def sum_1(u, q, g, x_first, size):
             cols = pl.ds(0, 2 * size)
             wait_1(u, x_first, 2 * size).wait_recv()
-            if x_first:
-
-                def total(zi):
-                    value = partial[u, pl.ds(start_of(True, x, zi), own), cols].astype(F32)
-                    for d in range(ranks_x - 1):
-                        at = pl.ds(aligned(d * 2 * own + zi * own, own), own)
-                        value = value + land_1[u, at, cols].astype(F32)
-                    return value
-
-                half_sum[u, pl.ds(0, own), cols] = total(1 - zh).astype(BF16)
-                remote(
-                    half_sum.at[u, pl.ds(0, own), cols],
-                    land_2.at[u, pl.ds(0, own), cols],
-                    ss_2.at[u],
-                    rs_2.at[u],
-                    z_peer,
-                ).start()
-                own_sum[u, :, cols] = total(zh)
-            else:
-                group = pl.ds(start_of(False, 0, zh), ranks_x * own)
-                got = pl.ds(0, ranks_x * own)
-                half_sum[u, got, cols] = (
-                    partial[u, group, cols].astype(F32) + land_1[u, got, cols].astype(F32)
-                ).astype(BF16)
-                for d in range(1, ranks_x):
-                    xi = x_peer(d)
+
+            def straight():
+                wait_2(u, x_first, 2 * size).wait_recv()
+                total = partial[u, pl.ds(start_of(x_first, x, zh), own), cols].astype(F32)
+                for _, _, _, land in slots(u, x_first, cols):
+                    total = total + land[...].astype(F32)
+                activate(u, q, total, x_first, size)
+
+            def stepwise():
+                if x_first:
+
+                    def total(zi):
+                        value = partial[u, pl.ds(start_of(True, x, zi), own), cols].astype(F32)
+                        for d in range(ranks_x - 1):
+                            at = pl.ds(aligned(d * 2 * own + zi * own, own), own)
+                            value = value + land_1[u, at, cols].astype(F32)
+                        return value
+
+                    half_sum[u, pl.ds(0, own), cols] = total(1 - zh).astype(BF16)
                     remote(
-                        half_sum.at[u, pl.ds(aligned(xi * own, own), own), cols],
-                        land_2.at[u, pl.ds((d - 1) * own, own), cols],
+                        half_sum.at[u, pl.ds(0, own), cols],
+                        land_2.at[u, pl.ds(0, own), cols],
                         ss_2.at[u],
                         rs_2.at[u],
-                        (w, xi * 2 + zh),
+                        z_peer,
                     ).start()
-                mine = pl.ds(aligned(x * own, own), own)
-                own_sum[u, :, cols] = (
-                    partial[u, pl.ds(start_of(False, x, zh), own), cols].astype(F32)
-                    + land_1[u, mine, cols].astype(F32)
-                )
+                    own_sum[u, :, cols] = total(zh)
+                else:
+                    group = pl.ds(start_of(False, 0, zh), ranks_x * own)
+                    got = pl.ds(0, ranks_x * own)
+                    half_sum[u, got, cols] = (
+                        partial[u, group, cols].astype(F32) + land_1[u, got, cols].astype(F32)
+                    ).astype(BF16)
+                    for d in range(1, ranks_x):
+                        xi = x_peer(d)
+                        remote(
+                            half_sum.at[u, pl.ds(aligned(xi * own, own), own), cols],
+                            land_2.at[u, pl.ds((d - 1) * own, own), cols],
+                            ss_2.at[u],
+                            rs_2.at[u],
+                            (w, xi * 2 + zh),
+                        ).start()
+                    mine = pl.ds(aligned(x * own, own), own)
+                    own_sum[u, :, cols] = (
+                        partial[u, pl.ds(start_of(False, x, zh), own), cols].astype(F32)
+                        + land_1[u, mine, cols].astype(F32)
+                    )
+
+            in_two_ways(q, g, straight, stepwise)
 
         def sum_2(u, q, g, x_first, size):
-            wait_2(u, x_first, 2 * size).wait_recv()
-            total = own_sum[u, :, pl.ds(0, 2 * size)]
-            for d in range(1 if x_first else ranks_x - 1):
-                total = total + land_2[u, pl.ds(d * own, own), pl.ds(0, 2 * size)].astype(F32)
-            activate(u, q, total, x_first, size)
+            def stepwise():
+                wait_2(u, x_first, 2 * size).wait_recv()
+                total = own_sum[u, :, pl.ds(0, 2 * size)]
+                for d in range(1 if x_first else ranks_x - 1):
+                    total = total + land_2[u, pl.ds(d * own, own), pl.ds(0, 2 * size)].astype(F32)
+                activate(u, q, total, x_first, size)
+
+            in_two_ways(q, g, lambda: None, stepwise)
 
         def wait_early(u, x_first, size):
             count = own if x_first else (ranks_x - 1) * own
@@ -405,9 +457,6 @@
                 core_send[q // 2] = acc[q, :, feats].astype(BF16)
                 core_copy(q // 2).start()
 
-        def out_copy(h, src, dst, send, recv, device):
-            return remote(src, dst, send.at[h], recv.at[h], device)
-
         def to_owners(q):
             h = q // 2
 
@@ -419,32 +468,13 @@
                 out_send[h] = both.astype(BF16)
                 for d in range(1, ranks_y):
                     yi = y_peer(d)
-                    if q < CHUNKS - 1:
-                        at = pl.ds((d - 1) * 2 * part, 2 * part)
-                        remote(
-                            out_send.at[h, tok_place(yi, 0, 2)],
-                            out_land.at[h, at],
-                            out_ss.at[h],
-                            out_rs.at[h],
-                            chip_at(yi, zl),
-                        ).start()
-                        continue
-                    for zi in range(2):
-                        at = pl.ds(aligned(((d - 1) * 2 + zl) * part, part), part)
-                        remote(
-                            out_send.at[h, tok_place(yi, zi)],
-                            out_land.at[h, at],
-                            out_ss.at[h],
-                            out_rs.at[h],
-                            chip_at(yi, zi),
-                        ).start()
-                if q == CHUNKS - 1:
+                    at = pl.ds((d - 1) * 2 * part, 2 * part)
                     remote(
-                        out_send.at[h, tok_place(y, 1 - zl)],
-                        z_land.at[h],
-                        z_ss.at[h],
-                        z_rs.at[h],
-                        chip_at(y, 1 - zl),
+                        out_send.at[h, tok_place(yi, 0, 2)],
+                        out_land.at[h, at],
+                        out_ss.at[h],
+                        out_rs.at[h],
+                        chip_at(yi, zl),
                     ).start()
 
         def out_wait(h):
@@ -478,10 +508,6 @@
             @pl.when(core == q % 2)
             def _():
                 total = acc[q, place, feats]
-                if q == CHUNKS - 1:
-                    out_wait(h).wait()
-                    for d in range((ranks_y - 1) * 2):
-                        total = total + out_land[h, pl.ds(d * part, part)].astype(F32)
                 z_copy(h).wait()
                 out[pl.ds(h * part, part), :] = total + z_land[h].astype(F32)
                 pair_copy(q).wait_send()
@@ -489,6 +515,82 @@
             @pl.when(core != q % 2)
             def _():
                 core_copy(h).wait_send()
+
+        last = CHUNKS - 1
+        last_h = last // 2
+        piece = depth // PIECES
+
+        def piece_copy(i):
+            at = pl.ds(i * piece, piece)
+            return remote(
+                core_send.at[last_h, :, at],
+                core_land.at[last_h, :, at],
+                piece_cs.at[i],
+                piece_cr.at[i],
+                sibling,
+            )
+
+        def piece_wait(i):
+            got = out_land.at[last_h, pl.ds(0, (chips - 2) * part), pl.ds(i * piece, piece)]
+            rest = z_land.at[last_h, :, pl.ds(i * piece, piece)]
+            return [
+                remote(got, got, piece_os.at[i], piece_or.at[i], sibling),
+                remote(rest, rest, piece_zs.at[i], piece_zr.at[i], sibling),
+            ]
+
+        def last_to_core():
+            low = acc[last, :, pl.ds(depth, LANE)].astype(BF16)
+            for i in range(PIECES):
+                at = pl.ds(i * piece, piece)
+                acc[last, :, at] += jnp.dot(low, dright_b[:, at], preferred_element_type=F32)
+
+                @pl.when(core != last % 2)
+                def _():
+                    core_send[last_h, :, at] = acc[last, :, at].astype(BF16)
+                    piece_copy(i).start()
+
+        def last_to_owners():
+            @pl.when(core == last % 2)
+            def _():
+                for i in range(PIECES):
+                    at = pl.ds(i * piece, piece)
+                    piece_copy(i).wait_recv()
+                    both = acc[last, :, at] + core_land[last_h, :, at].astype(F32)
+                    acc[last, :, at] = both
+                    out_send[last_h, :, at] = both.astype(BF16)
+
+                    def send(yi, zi, land, out_s=piece_os, out_r=piece_or):
+                        remote(
+                            out_send.at[last_h, tok_place(yi, zi), at],
+                            land,
+                            out_s.at[i],
+                            out_r.at[i],
+                            chip_at(yi, zi),
+                        ).start()
+
+                    for d in FAR_FIRST:
+                        here = pl.ds(aligned(((d - 1) * 2 + zl) * part, part), part)
+                        for zi in range(2):
+                            send(y_peer(d), zi, out_land.at[last_h, here, at])
+                    send(y, 1 - zl, z_land.at[last_h, :, at], piece_zs, piece_zr)
+
+        def last_finish():
+            @pl.when(core == last % 2)
+            def _():
+                for i in range(PIECES):
+                    at = pl.ds(i * piece, piece)
+                    for copy in piece_wait(i):
+                        copy.wait()
+                    total = acc[last, place, at] + z_land[last_h, :, at].astype(F32)
+                    for d in range(chips - 2):
+                        total = total + out_land[last_h, pl.ds(d * part, part), at].astype(F32)
+                    out[pl.ds(last_h * part, part), at] = total
+                pair_copy(last).wait_send()
+
+            @pl.when(core != last % 2)
+            def _():
+                for i in range(PIECES):
+                    piece_copy(i).wait_send()
 
         def scope(name, function, *given):
             with jax.named_scope(name):
@@ -541,17 +643,17 @@
                         for name, function, q in todo:
                             scope(name, function, q)
 
-        last = CHUNKS - 1
-        scope("to_owning_core", to_owning_core, last)
+        scope("to_owning_core", last_to_core)
         for name, function, q in late:
             if q % 2 != last % 2:
                 scope(name, function, q)
-        scope("to_owners", to_owners, last)
+        scope("to_owners", last_to_owners)
         for name, function, q in late:
             if q % 2 == last % 2:
                 scope(name, function, q)
-        for q in range(CHUNKS):
+        for q in range(CHUNKS - 1):
             scope("finish", finish, q)
+        scope("finish_last", last_finish)
 
     vmem = pltpu.VMEM
     dma = pltpu.SemaphoreType.DMA
@@ -589,6 +691,8 @@
         dma((units,)), dma((units,)), dma((units,)),
         dma((HALVES,)), dma((HALVES,)), dma((HALVES,)), dma((HALVES,)),
         dma((HALVES,)), dma((HALVES,)),
+        dma((PIECES,)), dma((PIECES,)), dma((PIECES,)), dma((PIECES,)),
+        dma((PIECES,)), dma((PIECES,)),
     ]
     return kernel, scratch
 

time: 79.7 us -> 82.3 us (1.033)
  Pallas kernels: 77.8 us -> 80.4 us
    pallas_call x1, Pallas kernels: 77.8 us -> 80.4 us  [shards(): pl.pallas_call(kernel, out_shape=jax.ShapeDtypeStruct((tok_rows, depth),...]
where the time goes in v4:
time: 82.3 us; the launch traced here: 82.1 us
  Pallas kernels  80.4 us (98%)
  local copies, waits for them, and re-layouts  1.67 us (2%)
    pallas_call x1, Pallas kernels, shards(): pl.pallas_call(kernel, out_shape=jax.ShapeDtypeStruct((tok_rows, depth),...  80.4 us
    unnamed x1, local copies, waits for them, and re-layouts  1.67 us

profile of v4, /device:TPU:1, one launch (start us, length us, event | category | flops | bytes accessed | tf_op | source)
XLA Modules:
  0.0 82.1 jit_solution(18191247606908938669)
XLA Ops:
  0.0 80.4 %shard_map.127 = f32[32,2048]{1,0:T(8,128)} custom-call(bf16[32,2048]{1,0:T(8,128)(2,1)} %tok.1, bf16[2048,1664]{1,0:T(8,128)(2,1)} %gate_codes.1, bf16[2048,1664]{1,0:T(8,128)(2,1)} %up_codes.1, f32[16,1664]{1,0:T(8,128)} %gate_scale.1, f32[16,1664]{1,0:T(8,128)} %up_scale.1, bf16[1664,2048]{1,0:T(8,128)(2,1)} %down_codes.1, f32[13,2048]{1,0:T(8,128)} %down_scale.1, ...), custom_call_target="tpu_custom_call" | custom-call | tf_op jit(solution)/shard_map/pallas_call | solution.py:710
  80.4 1.7 %copy.15 = f32[32,2048]{1,0:T(8,128)} copy(f32[32,2048]{1,0:T(8,128)} %shard_map.127) | data formatting | bytes 524288

commit v5 on v3

--- a/solution.py
+++ b/solution.py
@@ -17,7 +17,8 @@
 AFTER = (3, 9)
 OUT_AT = (-1, 0, 3)
 RELAY_AT = (-1, 4, 10)
-PAIR_AT = (1, 9, 16)
+PAIR_AT = (3, 9, 16)
+WINDOW = 14
 SPREAD = 3
 
 
@@ -59,7 +60,7 @@
         scale_v, dscale_v, left_v, right_v, dleft_v, dright_v, left_b, dright_b,
         load_w, load_d, load_s,
         tok_send, tok_first, tok_recv, tok_recv_z, pair_send, pair_recv,
-        ss_1, rs_1, ss_2, rs_2, hid_send, hid_recv_1, hid_recv_2,
+        unit_send, rs_1, rs_2, hid_recv_1, hid_recv_2,
         core_ss, core_rs, out_ss, out_rs, z_ss, z_rs,
     ):
         w = lax.axis_index("wide")
@@ -102,7 +103,7 @@
                 pltpu.make_async_copy(
                     codes.at[:, cols_of(g, size)],
                     target.at[feats, pl.ds(i * size, size)],
-                    load_w.at[i, g],
+                    load_w.at[g],
                 )
                 for i, codes in enumerate((gate_codes, up_codes))
             ]
@@ -110,7 +111,7 @@
         def down_load(g):
             here = pl.ds(aligned(g * LANE, LANE), LANE)
             return pltpu.make_async_copy(
-                down_codes.at[here, :], w_down.at[here, feats], load_d.at[g]
+                down_codes.at[here, :], w_down.at[here, feats], load_d.at[0]
             )
 
         with jax.named_scope("issue"):
@@ -217,8 +218,8 @@
             left_b[:, pl.ds(LANE, LANE)] = left_v[1].astype(BF16)
 
             def widen(g, target, size):
-                for copy in up_loads(g, target, size):
-                    copy.wait()
+                whole = target.at[feats, :]
+                pltpu.make_async_copy(whole, whole, load_w.at[g]).wait()
                 for i in range(2):
                     here = pl.ds(i * size, size)
                     for k in range(groups):
@@ -237,10 +238,11 @@
             for copy in small[6:]:
                 copy.wait()
             dright_b[...] = dright_v[...].astype(BF16)
+            whole = w_down.at[:, feats]
+            pltpu.make_async_copy(whole, whole, load_d.at[0]).wait()
 
             @pl.loop(0, blocks)
             def _(g):
-                down_load(g).wait()
                 here = pl.ds(aligned(g * LANE, LANE), LANE)
                 scale = dscale_v[pl.ds(g, 1), :]
                 w_down[here, feats] = (w_down[here, feats].astype(F32) * scale).astype(BF16)
@@ -252,17 +254,23 @@
         def start_of(x_first, xi, zi):
             return aligned(xi * 2 * own + zi * own if x_first else zi * ranks_x * own + xi * own, own)
 
-        def bytes_of(buffer, u, count, size, send, recv):
+        def slot(u):
+            return u - jnp.where(u >= WINDOW, WINDOW, 0)
+
+        def arrival(recv, u):
+            return recv.at[u if recv is hid_recv_2 else slot(u)]
+
+        def bytes_of(buffer, u, count, size, recv):
             at = buffer.at[u, pl.ds(0, count), pl.ds(0, size)]
-            return remote(at, at, send.at[u], recv.at[u], sibling)
+            return remote(at, at, unit_send.at[u], arrival(recv, u), sibling)
 
         def wait_1(u, x_first, size):
             count = (ranks_x - 1) * 2 * own if x_first else ranks_x * own
-            return bytes_of(land_1, u, count, size, ss_1, rs_1)
+            return bytes_of(land_1, u, count, size, rs_1)
 
         def wait_2(u, x_first, size):
             count = own if x_first else (ranks_x - 1) * own
-            return bytes_of(land_2, u, count, size, ss_2, rs_2)
+            return bytes_of(land_2, u, count, size, rs_2)
 
         def first(u, q, g, x_first, size):
             cols = pl.ds(0, 2 * size)
@@ -276,22 +284,22 @@
                     remote(
                         partial.at[u, pl.ds(start_of(True, xi, 0), 2 * own), cols],
                         land_1.at[u, pl.ds((d - 1) * 2 * own, 2 * own), cols],
-                        ss_1.at[u],
-                        rs_1.at[u],
+                        unit_send.at[u],
+                        rs_1.at[slot(u)],
                         (w, xi * 2 + zh),
                     ).start()
             else:
                 remote(
                     partial.at[u, pl.ds(start_of(False, 0, 1 - zh), ranks_x * own), cols],
                     land_1.at[u, pl.ds(0, ranks_x * own), cols],
-                    ss_1.at[u],
-                    rs_1.at[u],
+                    unit_send.at[u],
+                    rs_1.at[slot(u)],
                     z_peer,
                 ).start()
 
         def hidden_copy(u, at, size, recv, device):
             here = hidden.at[u, at, pl.ds(0, size)]
-            return remote(here, here, hid_send.at[u], recv.at[u], device)
+            return remote(here, here, unit_send.at[u], arrival(recv, u), device)
 
         def activate(u, q, total, x_first, size):
             gate, up = total[:, :size], total[:, size:]
@@ -326,8 +334,8 @@
                 remote(
                     half_sum.at[u, pl.ds(0, own), cols],
                     land_2.at[u, pl.ds(0, own), cols],
-                    ss_2.at[u],
-                    rs_2.at[u],
+                    unit_send.at[u],
+                    rs_2.at[slot(u)],
                     z_peer,
                 ).start()
                 own_sum[u, :, cols] = total(zh)
@@ -342,8 +350,8 @@
                     remote(
                         half_sum.at[u, pl.ds(aligned(xi * own, own), own), cols],
                         land_2.at[u, pl.ds((d - 1) * own, own), cols],
-                        ss_2.at[u],
-                        rs_2.at[u],
+                        unit_send.at[u],
+                        rs_2.at[slot(u)],
                         (w, xi * 2 + zh),
                     ).start()
                 mine = pl.ds(aligned(x * own, own), own)
@@ -361,11 +369,11 @@
 
         def wait_early(u, x_first, size):
             count = own if x_first else (ranks_x - 1) * own
-            return bytes_of(hidden, u, count, size, hid_send, hid_recv_1)
+            return bytes_of(hidden, u, count, size, hid_recv_1)
 
         def wait_late(u, x_first, size):
             count = (ranks_x - 1) * 2 * own if x_first else ranks_x * own
-            return bytes_of(hidden, u, count, size, hid_send, hid_recv_2)
+            return bytes_of(hidden, u, count, size, hid_recv_2)
 
         def relay(u, q, g, x_first, size):
             wait_early(u, x_first, size).wait_recv()
@@ -389,9 +397,8 @@
                 w_down[cols_of(g, size), :],
                 preferred_element_type=F32,
             )
-            wait_1(u, x_first, 2 * size).wait_send()
-            wait_2(u, x_first, 2 * size).wait_send()
-            bytes_of(hidden, u, (n_narrow - 1) * own, size, hid_send, hid_recv_2).wait_send()
+            sent = w_down.at[pl.ds(0, (n_narrow - 1) * own * 3), pl.ds(0, size)]
+            remote(sent, sent, unit_send.at[u], hid_recv_2.at[u], sibling).wait_send()
 
         def core_copy(h):
             return remote(core_send.at[h], core_land.at[h], core_ss.at[h], core_rs.at[h], sibling)
@@ -581,12 +588,12 @@
         vmem((LANE, depth), F32),
         vmem((depth, 2 * LANE), BF16),
         vmem((LANE, depth), BF16),
-        dma((2, UNITS)),
-        dma((blocks,)),
+        dma((UNITS,)),
+        dma((1,)),
         dma((9,)),
         dma((HALVES,)), dma((chips - 1,)), dma((HALVES,)), dma((HALVES,)), dma((CHUNKS,)), dma((CHUNKS,)),
-        dma((units,)), dma((units,)), dma((units,)), dma((units,)),
-        dma((units,)), dma((units,)), dma((units,)),
+        dma((units,)),
+        dma((WINDOW,)), dma((WINDOW,)), dma((WINDOW,)), dma((units,)),
         dma((HALVES,)), dma((HALVES,)), dma((HALVES,)), dma((HALVES,)),
         dma((HALVES,)), dma((HALVES,)),
     ]

time: 79.7 us -> 79.8 us (level)
  no operation moved by 1% of the time
where the time goes in v5:
time: 79.8 us; the launch traced here: 79.6 us
  Pallas kernels  77.9 us (98%)
  local copies, waits for them, and re-layouts  1.67 us (2%)
    pallas_call x1, Pallas kernels, shards(): pl.pallas_call(kernel, out_shape=jax.ShapeDtypeStruct((tok_rows, depth),...  77.9 us
    unnamed x1, local copies, waits for them, and re-layouts  1.67 us

profile of v5, /device:TPU:1, one launch (start us, length us, event | category | flops | bytes accessed | tf_op | source)
XLA Modules:
  0.0 79.6 jit_solution(4255452840601529094)
XLA Ops:
  0.0 77.9 %shard_map.127 = f32[32,2048]{1,0:T(8,128)} custom-call(bf16[32,2048]{1,0:T(8,128)(2,1)} %tok.1, bf16[2048,1664]{1,0:T(8,128)(2,1)} %gate_codes.1, bf16[2048,1664]{1,0:T(8,128)(2,1)} %up_codes.1, f32[16,1664]{1,0:T(8,128)} %gate_scale.1, f32[16,1664]{1,0:T(8,128)} %up_scale.1, bf16[1664,2048]{1,0:T(8,128)(2,1)} %down_codes.1, f32[13,2048]{1,0:T(8,128)} %down_scale.1, ...), custom_call_target="tpu_custom_call" | custom-call | tf_op jit(solution)/shard_map/pallas_call | solution.py:613
  77.9 1.7 %copy.15 = f32[32,2048]{1,0:T(8,128)} copy(f32[32,2048]{1,0:T(8,128)} %shard_map.127) | data formatting | bytes 524288

commit v6 on v5

--- a/solution.py
+++ b/solution.py
@@ -18,6 +18,7 @@
 OUT_AT = (-1, 0, 3)
 RELAY_AT = (-1, 4, 10)
 PAIR_AT = (3, 9, 16)
+FAR_FIRST = (2, 1, 3)
 WINDOW = 14
 SPREAD = 3
 
@@ -279,7 +280,7 @@
                 x_all[q], weights, preferred_element_type=F32
             ).astype(BF16)
             if x_first:
-                for d in range(1, ranks_x):
+                for d in FAR_FIRST:
                     xi = x_peer(d)
                     remote(
                         partial.at[u, pl.ds(start_of(True, xi, 0), 2 * own), cols],
@@ -308,13 +309,13 @@
             along_z = hid_recv_1 if x_first else hid_recv_2
             along_x = hid_recv_2 if x_first else hid_recv_1
             hidden_copy(u, mine, size, along_z, z_peer).start()
-            for d in range(1, ranks_x):
+            for d in FAR_FIRST:
                 xi = x_peer(d) * 2
                 hidden_copy(u, mine, size, along_x, (w, xi + zh)).start()
 
             @pl.when(q >= SPREAD)
             def _():
-                for d in range(1, ranks_x):
+                for d in FAR_FIRST:
                     device = (w, x_peer(d) * 2 + 1 - zh)
                     hidden_copy(u, mine, size, hid_recv_2, device).start()
 
@@ -345,7 +346,7 @@
                 half_sum[u, got, cols] = (
                     partial[u, group, cols].astype(F32) + land_1[u, got, cols].astype(F32)
                 ).astype(BF16)
-                for d in range(1, ranks_x):
+                for d in FAR_FIRST:
                     xi = x_peer(d)
                     remote(
                         half_sum.at[u, pl.ds(aligned(xi * own, own), own), cols],
@@ -380,7 +381,7 @@
 
             @pl.when(q < SPREAD)
             def _():
-                for d in range(1, ranks_x):
+                for d in FAR_FIRST:
                     xi = x_peer(d)
                     if x_first:
                         at = pl.ds(start_of(True, x, 1 - zh), own)

time: 79.8 us -> 79.4 us (level)
  no operation moved by 1% of the time
where the time goes in v6:
time: 79.4 us; the launch traced here: 79.3 us
  Pallas kernels  77.6 us (98%)
  local copies, waits for them, and re-layouts  1.67 us (2%)
    pallas_call x1, Pallas kernels, shards(): pl.pallas_call(kernel, out_shape=jax.ShapeDtypeStruct((tok_rows, depth),...  77.6 us
    unnamed x1, local copies, waits for them, and re-layouts  1.67 us

profile of v6, /device:TPU:1, one launch (start us, length us, event | category | flops | bytes accessed | tf_op | source)
XLA Modules:
  0.0 79.3 jit_solution(5124820968722531788)
XLA Ops:
  0.0 77.6 %shard_map.127 = f32[32,2048]{1,0:T(8,128)} custom-call(bf16[32,2048]{1,0:T(8,128)(2,1)} %tok.1, bf16[2048,1664]{1,0:T(8,128)(2,1)} %gate_codes.1, bf16[2048,1664]{1,0:T(8,128)(2,1)} %up_codes.1, f32[16,1664]{1,0:T(8,128)} %gate_scale.1, f32[16,1664]{1,0:T(8,128)} %up_scale.1, bf16[1664,2048]{1,0:T(8,128)(2,1)} %down_codes.1, f32[13,2048]{1,0:T(8,128)} %down_scale.1, ...), custom_call_target="tpu_custom_call" | custom-call | tf_op jit(solution)/shard_map/pallas_call | solution.py:614
  77.6 1.7 %copy.15 = f32[32,2048]{1,0:T(8,128)} copy(f32[32,2048]{1,0:T(8,128)} %shard_map.127) | data formatting | bytes 524288
